TPU v7x, 32 devices: a whole 2x2x4 slice. The times are simulated.
32 devices in a mesh: lat: 2 (over x), lon: 16 (over z, y, core).
Axes of the slice: x: 2, y: 2, z: 4, core: 2. Of those that a mesh axis runs over, the one named last changes fastest.
Arguments:
- field: bfloat16 [128, 512, 128], P('lat', 'lon'), may hold values from -6 to 6
- land_mask: int32 [128, 512], P('lat', 'lon'), may hold values 0 or 1
- zonal_tap_weight: float32 [15, 128], replicated, may hold values from -1.5 to 1.5
- norm_gain: float32 [128], replicated, may hold values from 0.1 to 1.9
- up_weight: bfloat16 [128, 512], replicated, may hold values from -0.5 to 0.5
- down_weight: bfloat16 [512, 128], replicated, may hold values from -0.25 to 0.25
- polar_rows: int32 [64], P('lat'), may hold values from 0 to 63, as said below
- polar_owner: int32 [64], P('lat'), may hold values from 0 to 15, as said below
- polar_taps: float32 [31], replicated, may hold values from -0.8 to 0.8
Outputs:
- mixed_field: bfloat16 [128, 512, 128], P('lat', 'lon')
- polar_field: bfloat16 [128, 512, 128], P(('lat', 'lon'))
Inputs may be any that keep to these rules, and one draw needn't show every extreme that they name: `polar_rows`: within each band the 32 entries are distinct rows in increasing order. `polar_owner`: within each band no owner is named by more than 4 entries, and some owner by exactly 4.
All inputs are finite; a program needn't handle non-finite values. No bound on the sum of `land_mask` on one device may be relied on, other than what follows from the above.
Results may differ from a plain program's by a relative error of at most 0.0059.
Values may be sent and summed in bfloat16 or wider, within the bound.
No kernel may reach another device: no remote copies, remote signals or barrier semaphores. Data moves between devices by JAX's collectives and lax.ppermute only.
A program may use at most 64 MiB of HBM per device.

v0:
```python
import functools

import jax
import jax.numpy as jnp
from jax import lax
from jax.experimental import pallas as pl
from jax.experimental.pallas import tpu as pltpu
from jax.sharding import PartitionSpec as P

DILATION_STEP = 4
EXTRA = 16
VMEM_BYTES = 48 * 1024 * 1024
F32 = jnp.float32
BF16 = jnp.bfloat16


def spread_mask(mask_rows, channels):
    n, cols = mask_rows.shape
    eye = (
        lax.broadcasted_iota(jnp.int32, (cols, cols), 0)
        == lax.broadcasted_iota(jnp.int32, (cols, cols), 1)
    ).astype(F32)
    picked = (mask_rows[:, None, :] * eye[None]).astype(BF16).reshape(n * cols, cols)
    return jnp.dot(picked, jnp.ones((cols, channels), BF16), preferred_element_type=F32)


def branch_rows(triples, taps, gain, up, down):
    zonal = []
    n_taps = len(taps)
    for left, own, right in triples:
        cols = own.shape[0]
        start = cols - n_taps // 2 * DILATION_STEP
        line = jnp.concatenate([left, own, right], axis=0).astype(F32)
        aligned = shifted = None
        for k in range(n_taps):
            at = start + k * DILATION_STEP
            if at % 8 == 0:
                term = line[at : at + cols] * taps[k]
                aligned = term if aligned is None else aligned + term
            else:
                term = line[at - 4 : at - 4 + cols + 8] * taps[k]
                shifted = term if shifted is None else shifted + term
        zonal.append(aligned + shifted[4 : 4 + cols])
    zonal = jnp.concatenate(zonal, axis=0)
    mean = jnp.mean(zonal, axis=-1, keepdims=True)
    centred = zonal - mean
    var = jnp.mean(centred * centred, axis=-1, keepdims=True)
    normed = (centred * lax.rsqrt(var + 1e-6) * gain).astype(BF16)
    pre = jnp.dot(normed, up, preferred_element_type=F32)
    inner = pre * (0.7978845608028654 + (0.7978845608028654 * 0.044715) * (pre * pre))
    twice = (pre + pre * jnp.tanh(inner)).astype(BF16)
    return jnp.dot(twice, down, preferred_element_type=F32) * 0.5


def prep_kernel(
    slots, rows_ref, owner_ref, field_hbm, mask_ref, masked_ref, out_hbm,
    count, field, mask_f, extra, extra_half, load_sems, row_sems, extra_sem,
):
    lat_rows, cols, channels = field.shape
    tiles = out_hbm.shape[0]
    parts = load_sems.shape[0]
    some = lat_rows // parts
    entries = owner_ref.shape[0]
    loads = [
        pltpu.make_async_copy(field_hbm.at[pl.ds(p * some, some)], field.at[pl.ds(p * some, some)], load_sems.at[p])
        for p in range(parts)
    ]
    for load in loads:
        load.start()
    mask = mask_ref[...].astype(F32).T
    mask_f[...] = jnp.zeros_like(mask_f)
    mask_f[:, :cols] = mask
    extra[...] = jnp.zeros_like(extra)
    for tile in range(tiles):
        count[tile] = 0

    def row_copy(e, row, owner, rank):
        return pltpu.make_async_copy(
            field_hbm.at[row],
            out_hbm.at[owner, pl.ds(pl.multiple_of(rank * cols, cols), cols)],
            row_sems.at[e],
        )

    for e in range(entries):
        owner = owner_ref[e]
        row = rows_ref[e]
        rank = count[owner]
        count[owner] = rank + 1
        row_copy(e, row, owner, rank).start()
        extra[pl.ds(owner * EXTRA + rank, 1), :] = mask_f[pl.ds(row, 1), :]
    extra_half[...] = extra[...].astype(BF16).reshape(tiles, EXTRA, channels)
    extra_copy = pltpu.make_async_copy(extra_half, out_hbm.at[:, pl.ds(slots * cols, EXTRA)], extra_sem)
    extra_copy.start()
    for p, load in enumerate(loads):
        at = slice(p * some, (p + 1) * some)
        wide = spread_mask(mask[at], channels).astype(BF16)
        load.wait()
        masked_ref[at] = field[at] * wide.reshape(some, cols, channels)
    for e in range(entries):
        row_copy(e, 0, 0, 0).wait()
    extra_copy.wait()


def prep(field, land_mask, polar_rows, polar_owner, tiles, slots):
    lat_rows, cols, channels = field.shape
    smem = pl.BlockSpec(memory_space=pltpu.SMEM)
    vmem = pl.BlockSpec(memory_space=pltpu.VMEM)
    hbm = pl.BlockSpec(memory_space=pltpu.HBM)
    return pl.pallas_call(
        functools.partial(prep_kernel, slots),
        out_shape=(
            jax.ShapeDtypeStruct(field.shape, BF16),
            jax.ShapeDtypeStruct((tiles, slots * cols + EXTRA, channels), BF16),
        ),
        in_specs=[smem, smem, hbm, vmem],
        out_specs=(vmem, hbm),
        scratch_shapes=[
            pltpu.SMEM((tiles,), jnp.int32),
            pltpu.VMEM(field.shape, BF16),
            pltpu.VMEM((lat_rows, channels), F32),
            pltpu.VMEM((tiles * EXTRA, channels), F32),
            pltpu.VMEM((tiles, EXTRA, channels), BF16),
            pltpu.SemaphoreType.DMA((4,)),
            pltpu.SemaphoreType.DMA(polar_owner.shape),
            pltpu.SemaphoreType.DMA,
        ],
        compiler_params=pltpu.CompilerParams(vmem_limit_bytes=VMEM_BYTES),
        cost_estimate=pl.CostEstimate(flops=10**6, bytes_accessed=2 * 10**6, transcendentals=0),
        name="prep",
    )(polar_rows, polar_owner, field, land_mask.T)


def tile_kernel(
    chunk, polar_taps_ref, own_ref, cross_ref, swap_ref, mask_ref, taps_ref, gain_ref, up_ref, down_ref,
    mixed_ref, high_ref, low_ref, left, right, mask_f,
):
    lat_rows, cols, channels = own_ref.shape
    me = lax.axis_index("lon")
    odd = lax.rem(me, 2)

    @pl.when(odd == 0)
    def _():
        left[...] = cross_ref[...]
        right[...] = swap_ref[...]

    @pl.when(odd == 1)
    def _():
        left[...] = swap_ref[...]
        right[...] = cross_ref[...]

    mask_f[...] = mask_ref[...].astype(F32).T

    def some_rows(step, _):
        at = pl.ds(step * chunk, chunk)
        triples = [(left[step * chunk + r], own_ref[step * chunk + r], right[step * chunk + r]) for r in range(chunk)]
        taps = [taps_ref[k : k + 1] for k in range(taps_ref.shape[0])]
        branch = branch_rows(triples, taps, gain_ref[...], up_ref[...], down_ref[...])
        wide = spread_mask(mask_f[at, :], channels)
        own = own_ref[at].reshape(chunk * cols, channels).astype(F32)
        mixed = wide * (own + branch.astype(BF16).astype(F32))
        mixed_ref[at] = mixed.astype(BF16).reshape(chunk, cols, channels)
        return 0

    lax.fori_loop(0, lat_rows // chunk, some_rows, 0)

    n, depth = high_ref.shape
    n_taps = polar_taps_ref.shape[0]
    offset = lax.broadcasted_iota(jnp.int32, (n, depth), 1) - lax.broadcasted_iota(jnp.int32, (n, depth), 0)
    first = (depth - n) // 2 - n_taps // 2
    band = jnp.zeros((n, depth), F32)
    for k in range(n_taps):
        band = jnp.where(offset == k + first, polar_taps_ref[k], band)
    high = band.astype(BF16)
    high_ref[...] = high
    low_ref[...] = (band - high.astype(F32)).astype(BF16)


def tile_part(polar_taps, masked, cross, swap, land_mask, weights):
    lat_rows, cols, channels = masked.shape
    smem = pl.BlockSpec(memory_space=pltpu.SMEM)
    vmem = pl.BlockSpec(memory_space=pltpu.VMEM)
    return pl.pallas_call(
        functools.partial(tile_kernel, 32),
        out_shape=(
            jax.ShapeDtypeStruct(masked.shape, BF16),
            jax.ShapeDtypeStruct((128, 160), BF16),
            jax.ShapeDtypeStruct((128, 160), BF16),
        ),
        in_specs=[smem] + [vmem] * 8,
        out_specs=(vmem, vmem, vmem),
        scratch_shapes=[pltpu.VMEM(masked.shape, BF16)] * 2 + [pltpu.VMEM((lat_rows, cols), F32)],
        compiler_params=pltpu.CompilerParams(vmem_limit_bytes=VMEM_BYTES),
        cost_estimate=pl.CostEstimate(flops=5 * 10**9, bytes_accessed=3 * 10**6, transcendentals=10**6),
        name="tile",
    )(polar_taps, masked, cross, swap, land_mask.T, *weights)


def polar_kernel(
    slots, cols, recv_ref, high_ref, low_ref, taps_ref, gain_ref, up_ref, down_ref,
    out_hbm, circle, out, sems,
):
    tiles, _, channels = recv_ref.shape
    n, depth = high_ref.shape
    pad = (depth - n) // 2
    nlon = tiles * cols
    taps = [taps_ref[k : k + 1] for k in range(taps_ref.shape[0])]
    extra = recv_ref[:, slots * cols :, :].astype(F32)
    copies = []
    for slot in range(slots):
        wide = spread_mask(extra[:, slot, :cols], channels)
        recv = jnp.concatenate([recv_ref[t, slot * cols : (slot + 1) * cols, :] for t in range(tiles)], axis=0)
        own = jnp.where(wide > 0.5, recv.astype(F32), 0.0)
        pieces = [own[t * cols : (t + 1) * cols] for t in range(tiles)]
        triples = [(pieces[t - 1], pieces[t], pieces[(t + 1) % tiles]) for t in range(tiles)]
        branch = branch_rows(triples, taps, gain_ref[...], up_ref[...], down_ref[...])
        mixed = (wide * (own + branch.astype(BF16).astype(F32))).astype(BF16)
        circle[slot, pad : nlon + pad, :] = mixed
        circle[slot, :pad, :] = mixed[nlon - pad :]
        circle[slot, nlon + pad :, :] = mixed[:pad]
        for b in range(nlon // n):
            window = circle[slot, b * n : b * n + depth, :]
            out[slot, b * n : (b + 1) * n, :] = (
                jnp.dot(high_ref[...], window, preferred_element_type=F32)
                + jnp.dot(low_ref[...], window, preferred_element_type=F32)
            ).astype(BF16)
        copies.append(pltpu.make_async_copy(out.at[slot], out_hbm.at[slot], sems.at[slot]))
        copies[-1].start()
    for copy in copies:
        copy.wait()


def polar_part(recv, high, low, weights, slots, cols):
    tiles, _, channels = recv.shape
    vmem = pl.BlockSpec(memory_space=pltpu.VMEM)
    shape = (slots, tiles * cols, channels)
    return pl.pallas_call(
        functools.partial(polar_kernel, slots, cols),
        out_shape=jax.ShapeDtypeStruct(shape, BF16),
        in_specs=[vmem] * 7,
        out_specs=pl.BlockSpec(memory_space=pltpu.HBM),
        scratch_shapes=[
            pltpu.VMEM((slots, tiles * cols + 32, channels), BF16),
            pltpu.VMEM(shape, BF16),
            pltpu.SemaphoreType.DMA((slots,)),
        ],
        compiler_params=pltpu.CompilerParams(vmem_limit_bytes=VMEM_BYTES),
        cost_estimate=pl.CostEstimate(flops=6 * 10**8, bytes_accessed=2 * 10**6, transcendentals=10**6),
        name="polar",
    )(recv, high, low, *weights)


def body(
    field,
    land_mask,
    zonal_tap_weight,
    norm_gain,
    up_weight,
    down_weight,
    polar_rows,
    polar_owner,
    polar_taps,
):
    lat_rows, cols, channels = field.shape
    tiles = lax.axis_size("lon")
    slots = max(2, lat_rows // tiles)
    weights = (
        zonal_tap_weight,
        norm_gain.reshape(1, channels),
        up_weight,
        down_weight,
    )
    masked, outgoing = prep(field, land_mask, polar_rows, polar_owner, tiles, slots)
    swap_pairs = [(i, i ^ 1) for i in range(tiles)]
    cross_pairs = [(i, (i + 1) % tiles if i % 2 else (i - 1) % tiles) for i in range(tiles)]
    cross = lax.ppermute(masked, "lon", cross_pairs)
    swap = lax.ppermute(masked, "lon", swap_pairs)
    recv = lax.all_to_all(outgoing, "lon", split_axis=0, concat_axis=0, tiled=True)
    mixed, high, low = tile_part(polar_taps, masked, cross, swap, land_mask, weights)
    polar = polar_part(recv, high, low, weights, slots, cols)
    return (mixed, polar)


def solution(mesh):
    in_specs = (P("lat", "lon", None), P("lat", "lon"), P(), P(), P(), P(), P("lat"), P("lat"), P())
    out_specs = (P("lat", "lon", None), P(("lat", "lon"), None, None))
    return jax.shard_map(body, mesh=mesh, in_specs=in_specs, out_specs=out_specs, check_vma=False)
```

profile of v0, /device:TPU:0, one launch (start us, length us, event | category | flops | bytes accessed | tf_op | source)
XLA Modules:
  0.0 44.4 jit_solution(4555703256478684025)
XLA Ops:
  0.6 0.0 copy-start.4
  0.6 0.0 copy-start.3
  0.6 0.6 %copy-done.4 = s32[32]{0:T(128)S(1)} copy-done((s32[32]{0:T(128)S(1)}, s32[32]{0:T(128)}, u32[]{:S(2)}) %copy-start.4) | copy-done | bytes 152
  1.3 0.0 copy-done.3
  1.3 0.0 copy-start
  1.3 1.0 %copy-done = bf16[64,32,128]{2,1,0:T(8,128)(2,1)S(1)} copy-done((bf16[64,32,128]{2,1,0:T(8,128)(2,1)S(1)}, bf16[64,32,128]{2,1,0:T(8,128)(2,1)}, u32[]{:S(2)}) %copy-start) | copy-done | bytes 524312
  2.3 0.0 copy-start.1
  2.3 0.7 %copy-done.1 = s32[64,32]{0,1:T(8,128)S(1)} copy-done((s32[64,32]{0,1:T(8,128)S(1)}, s32[64,32]{0,1:T(8,128)}, u32[]{:S(2)}) %copy-start.1) | copy-done | bytes 8216
  3.1 2.5 %prep.1 = (bf16[64,32,128]{2,1,0:T(8,128)(2,1)S(1)}, bf16[16,144,128]{2,1,0:T(8,128)(2,1)}) custom-call(s32[32]{0:T(128)S(1)} %copy-done.3, s32[32]{0:T(128)S(1)} %copy-done.4, bf16[64,32,128]{2,1,0:T(8,128)(2,1)S(1)} %copy-done, s32[32,64]{1,0:T(8,128)S(1)} %bitcast.2), custom_call_target="tpu_custom_call" | custom-call | flops 1000000 | bytes 2000000 | tf_op jit(solution)/shard_map/prep/pallas_call | solution.py:109
  5.6 0.0 copy-start.2
  5.6 0.0 copy-start.5
  5.6 0.0 copy-start.6
  5.6 0.0 copy-start.7
  5.6 7.5 %all-to-all-start = ((bf16[16,144,128]{2,1,0:T(8,128)(2,1)}), bf16[16,144,128]{2,1,0:T(8,128)(2,1)S(1)}, u32[]{:S(2)}, u32[]{:S(2)}) async-start(bf16[16,144,128]{2,1,0:T(8,128)(2,1)} %get-tuple-element.9), calls=%async_computation | async-start | bytes 1179648 | tf_op jit(solution)/shard_map/all_to_all | solution.py:277
  13.2 0.0 copy-start.8
  13.2 0.0 copy-start.9
  13.2 0.5 %collective-permute-start.1 = (bf16[64,32,128]{2,1,0:T(8,128)(2,1)S(1)}, bf16[64,32,128]{2,1,0:T(8,128)(2,1)S(1)}, u32[]{:S(2)}, u32[]{:S(2)}) collective-permute-start(bf16[64,32,128]{2,1,0:T(8,128)(2,1)S(1)} %get-tuple-element.7.own_ref), channel_id=1, source_target_pairs={{0,1},{1,0},{2,3},{3,2},{4,5},{5,4},{6,7},{7,6},{8,9},{9,8},{10,11... | collective-permute-start | bytes 1572872 | tf_op jit(solution)/shard_map/ppermute | solution.py:276
  13.7 4.3 %collective-permute-start = (bf16[64,32,128]{2,1,0:T(8,128)(2,1)S(1)}, bf16[64,32,128]{2,1,0:T(8,128)(2,1)S(1)}, u32[]{:S(2)}, u32[]{:S(2)}) collective-permute-start(bf16[64,32,128]{2,1,0:T(8,128)(2,1)S(1)} %get-tuple-element.7.own_ref), channel_id=1, source_target_pairs={{0,15},{1,2},{2,1},{3,4},{4,3},{5,6},{6,5},{7,8},{8,7},{9,10},{10,... | collective-permute-start | bytes 1572872 | tf_op jit(solution)/shard_map/ppermute | solution.py:275
  18.0 0.0 collective-permute-done.1.swap_ref
  18.0 16.3 %collective-permute-done.cross_ref = bf16[64,32,128]{2,1,0:T(8,128)(2,1)S(1)} collective-permute-done((bf16[64,32,128]{2,1,0:T(8,128)(2,1)S(1)}, bf16[64,32,128]{2,1,0:T(8,128)(2,1)S(1)}, u32[]{:S(2)}, u32[]{:S(2)}) %collective-permute-start) | collective-permute-done | bytes 524320 | tf_op jit(solution)/shard_map/ppermute | solution.py:275
  34.3 0.0 copy-done.2
  34.3 0.0 copy-done.5
  34.3 0.0 copy-done.6
  34.3 0.0 copy-done.7
  34.3 0.0 copy-done.8
  34.4 0.0 copy-done.9
  34.4 4.7 %tile.1 = (bf16[64,32,128]{2,1,0:T(8,128)(2,1)}, bf16[128,160]{1,0:T(8,128)(2,1)S(1)}, bf16[128,160]{1,0:T(8,128)(2,1)S(1)}) custom-call(f32[31]{0:T(128)S(1)} %copy-done.8, bf16[64,32,128]{2,1,0:T(8,128)(2,1)S(1)} %get-tuple-element.7.own_ref, bf16[64,32,128]{2,1,0:T(8,128)(2,1)S(1)} %collective-permute-done.cross_ref, ...), custom_call_target="tpu_custom_call" | custom-call | flops 5000000000 | bytes 3000000 | tf_op jit(solution)/shard_map/tile/pallas_call | solution.py:182
  39.1 0.0 all-to-all-done.recv_ref
  39.1 5.3 %polar.1 = bf16[4,512,128]{2,1,0:T(8,128)(2,1)} custom-call(bf16[16,144,128]{2,1,0:T(8,128)(2,1)S(1)} %all-to-all-done.recv_ref, bf16[128,160]{1,0:T(8,128)(2,1)S(1)} %get-tuple-element.10.high_ref, bf16[128,160]{1,0:T(8,128)(2,1)S(1)} %get-tuple-element.11.low_ref, f32[15,128]{1,0:T(8,128)S(1)} %copy-done.7, f32[1,128]{1,0:T(1,128)S(1)} %bitcast.5, ...), custom_call_target="tpu_custom_call" | custom-call | flops 600000000 | bytes 2000000 | tf_op jit(solution)/shard_map/polar/pallas_call | solution.py:236
Async XLA Ops:
  0.6 0.7 %copy-start.4 = (s32[32]{0:T(128)S(1)}, s32[32]{0:T(128)}, u32[]{:S(2)}) copy-start(s32[32]{0:T(128)} %owner_ref.1) | copy-start | bytes 388
  0.6 0.7 %copy-start.3 = (s32[32]{0:T(128)S(1)}, s32[32]{0:T(128)}, u32[]{:S(2)}) copy-start(s32[32]{0:T(128)} %rows_ref.1) | copy-start | bytes 388
  1.3 1.0 %copy-start = (bf16[64,32,128]{2,1,0:T(8,128)(2,1)S(1)}, bf16[64,32,128]{2,1,0:T(8,128)(2,1)}, u32[]{:S(2)}) copy-start(bf16[64,32,128]{2,1,0:T(8,128)(2,1)} %field_hbm.1) | copy-start | bytes 1572868
  2.3 0.7 %copy-start.1 = (s32[64,32]{0,1:T(8,128)S(1)}, s32[64,32]{0,1:T(8,128)}, u32[]{:S(2)}) copy-start(s32[64,32]{0,1:T(8,128)} %param.10) | copy-start | bytes 24580
  5.6 28.8 %copy-start.2 = (s32[64,32]{0,1:T(8,128)S(1)}, s32[64,32]{0,1:T(8,128)}, u32[]{:S(2)}) copy-start(s32[64,32]{0,1:T(8,128)} %param.10) | copy-start | bytes 24580
  5.6 28.7 %copy-start.5 = (bf16[128,512]{1,0:T(8,128)(2,1)S(1)}, bf16[128,512]{1,0:T(8,128)(2,1)}, u32[]{:S(2)}) copy-start(bf16[128,512]{1,0:T(8,128)(2,1)} %up_ref.3) | copy-start | bytes 393220
  5.6 28.7 %copy-start.6 = (bf16[512,128]{1,0:T(8,128)(2,1)S(1)}, bf16[512,128]{1,0:T(8,128)(2,1)}, u32[]{:S(2)}) copy-start(bf16[512,128]{1,0:T(8,128)(2,1)} %down_ref.3) | copy-start | bytes 393220
  5.6 28.7 %copy-start.7 = (f32[15,128]{1,0:T(8,128)S(1)}, f32[15,128]{1,0:T(8,128)}, u32[]{:S(2)}) copy-start(f32[15,128]{1,0:T(8,128)} %taps_ref.3) | copy-start | bytes 23044
  5.6 33.5 %all-to-all-start = ((bf16[16,144,128]{2,1,0:T(8,128)(2,1)}), bf16[16,144,128]{2,1,0:T(8,128)(2,1)S(1)}, u32[]{:S(2)}, u32[]{:S(2)}) async-start(bf16[16,144,128]{2,1,0:T(8,128)(2,1)} %get-tuple-element.9), calls=%async_computation | async-start | bytes 1179648 | tf_op jit(solution)/shard_map/all_to_all | solution.py:277
  13.2 21.2 %copy-start.8 = (f32[31]{0:T(128)S(1)}, f32[31]{0:T(128)}, u32[]{:S(2)}) copy-start(f32[31]{0:T(128)} %polar_taps_ref.1) | copy-start | bytes 376
  13.2 21.2 %copy-start.9 = (f32[128]{0:T(128)S(1)}, f32[128]{0:T(128)}, u32[]{:S(2)}) copy-start(f32[128]{0:T(128)} %param.12) | copy-start | bytes 1540
  13.2 4.8 %collective-permute-start.1 = (bf16[64,32,128]{2,1,0:T(8,128)(2,1)S(1)}, bf16[64,32,128]{2,1,0:T(8,128)(2,1)S(1)}, u32[]{:S(2)}, u32[]{:S(2)}) collective-permute-start(bf16[64,32,128]{2,1,0:T(8,128)(2,1)S(1)} %get-tuple-element.7.own_ref), channel_id=1, source_target_pairs={{0,1},{1,0},{2,3},{3,2},{4,5},{5,4},{6,7},{7,6},{8,9},{9,8},{10,11... | collective-permute-start | bytes 1572872 | tf_op jit(solution)/shard_map/ppermute | solution.py:276
  13.7 20.7 %collective-permute-start = (bf16[64,32,128]{2,1,0:T(8,128)(2,1)S(1)}, bf16[64,32,128]{2,1,0:T(8,128)(2,1)S(1)}, u32[]{:S(2)}, u32[]{:S(2)}) collective-permute-start(bf16[64,32,128]{2,1,0:T(8,128)(2,1)S(1)} %get-tuple-element.7.own_ref), channel_id=1, source_target_pairs={{0,15},{1,2},{2,1},{3,4},{4,3},{5,6},{6,5},{7,8},{8,7},{9,10},{10,... | collective-permute-start | bytes 1572872 | tf_op jit(solution)/shard_map/ppermute | solution.py:275
where the time goes:
time: 44.8 us; the launch traced here: 44.4 us
  waiting for transfers between devices  16.3 us (36%)
  Pallas kernels  12.6 us (28%)
  starting transfers between devices  12.3 us (27%)
  local copies, waits for them, and re-layouts  2.45 us (5%)
  between operations  0.74 us (2%)
    ppermute x1, waiting for transfers between devices, body(): cross = lax.ppermute(masked, 'lon', cross_pairs)  16.3 us
    all_to_all x1, starting transfers between devices, body(): lax.all_to_all(outgoing, 'lon', split_axis=0, concat_axis=0, tiled=True)  7.53 us
    pallas_call x1, Pallas kernels, polar_part(): pl.pallas_call(functools.partial(polar_kernel, slots, cols), out_shape=ja...  5.32 us
    pallas_call x1, Pallas kernels, tile_part(): pl.pallas_call(functools.partial(tile_kernel, 32), out_shape=(jax.ShapeDt...  4.74 us
    ppermute x1, starting transfers between devices, body(): cross = lax.ppermute(masked, 'lon', cross_pairs)  4.33 us
    pallas_call x1, Pallas kernels, prep(): pl.pallas_call(functools.partial(prep_kernel, slots), out_shape=(jax.Shap...  2.51 us
    unnamed x20, local copies, waits for them, and re-layouts  2.45 us
  transfers between devices with their start and end apart: 3, of which 1 were waited for; matrix products, arithmetic and copies ran while one was open for 0% of the time, Pallas kernels for 11%

commit v1 on v0

--- a/solution.py
+++ b/solution.py
@@ -76,18 +76,19 @@
 
     def row_copy(e, row, owner, rank):
         return pltpu.make_async_copy(
-            field_hbm.at[row],
+            masked_ref.at[row],
             out_hbm.at[owner, pl.ds(pl.multiple_of(rank * cols, cols), cols)],
             row_sems.at[e],
         )
 
+    places = []
     for e in range(entries):
         owner = owner_ref[e]
         row = rows_ref[e]
         rank = count[owner]
         count[owner] = rank + 1
-        row_copy(e, row, owner, rank).start()
         extra[pl.ds(owner * EXTRA + rank, 1), :] = mask_f[pl.ds(row, 1), :]
+        places.append((row, owner, rank))
     extra_half[...] = extra[...].astype(BF16).reshape(tiles, EXTRA, channels)
     extra_copy = pltpu.make_async_copy(extra_half, out_hbm.at[:, pl.ds(slots * cols, EXTRA)], extra_sem)
     extra_copy.start()
@@ -96,8 +97,10 @@
         wide = spread_mask(mask[at], channels).astype(BF16)
         load.wait()
         masked_ref[at] = field[at] * wide.reshape(some, cols, channels)
-    for e in range(entries):
-        row_copy(e, 0, 0, 0).wait()
+    for e, place in enumerate(places):
+        row_copy(e, *place).start()
+    for e, place in enumerate(places):
+        row_copy(e, *place).wait()
     extra_copy.wait()
 
 
@@ -124,7 +127,6 @@
             pltpu.SemaphoreType.DMA(polar_owner.shape),
             pltpu.SemaphoreType.DMA,
         ],
-        compiler_params=pltpu.CompilerParams(vmem_limit_bytes=VMEM_BYTES),
         cost_estimate=pl.CostEstimate(flops=10**6, bytes_accessed=2 * 10**6, transcendentals=0),
         name="prep",
     )(polar_rows, polar_owner, field, land_mask.T)
@@ -190,7 +192,7 @@
         out_specs=(vmem, vmem, vmem),
         scratch_shapes=[pltpu.VMEM(masked.shape, BF16)] * 2 + [pltpu.VMEM((lat_rows, cols), F32)],
         compiler_params=pltpu.CompilerParams(vmem_limit_bytes=VMEM_BYTES),
-        cost_estimate=pl.CostEstimate(flops=5 * 10**9, bytes_accessed=3 * 10**6, transcendentals=10**6),
+        cost_estimate=pl.CostEstimate(flops=5 * 10**10, bytes_accessed=3 * 10**6, transcendentals=10**6),
         name="tile",
     )(polar_taps, masked, cross, swap, land_mask.T, *weights)
 

time: 44.8 us -> 36 us (0.80)
  waiting for transfers between devices: 16.3 us -> 10.7 us
  local copies, waits for them, and re-layouts: 2.45 us -> 0.03 us
  starting transfers between devices: 12.3 us -> 9.91 us
  Pallas kernels: 12.6 us -> 14.4 us
    ppermute x1, waiting for transfers between devices: 16.3 us -> 5.47 us  [body(): cross = lax.ppermute(masked, 'lon', cross_pairs)]
    all_to_all x1, waiting for transfers between devices: 0.01 us -> 5.2 us  [body(): lax.all_to_all(outgoing, 'lon', split_axis=0, concat_axis=0, tiled=True)]
    all_to_all x1, starting transfers between devices: 7.53 us -> 3.73 us  [body(): lax.all_to_all(outgoing, 'lon', split_axis=0, concat_axis=0, tiled=True)]
    unnamed x20 -> x14, local copies, waits for them, and re-layouts: 2.45 us -> 0.03 us
    pallas_call x1, Pallas kernels: 2.51 us -> 4.29 us  [prep(): pl.pallas_call(functools.partial(prep_kernel, slots), out_shape=(jax.Shap...]
    ppermute x1, starting transfers between devices: 4.33 us -> 5.66 us  [body(): cross = lax.ppermute(masked, 'lon', cross_pairs)]
  transfers between devices with their start and end apart: 3 -> 3, of which waited for: 1 -> 2; matrix products, arithmetic and copies ran while one was open for 0% -> 0% of each run, Pallas kernels for 11% -> 13%
where the time goes in v1:
time: 36 us; the launch traced here: 35.7 us
  Pallas kernels  14.4 us (40%)
  waiting for transfers between devices  10.7 us (30%)
  starting transfers between devices  9.91 us (28%)
  between operations  0.71 us (2%)
    ppermute x1, starting transfers between devices, body(): cross = lax.ppermute(masked, 'lon', cross_pairs)  5.66 us
    ppermute x1, waiting for transfers between devices, body(): cross = lax.ppermute(masked, 'lon', cross_pairs)  5.47 us
    pallas_call x1, Pallas kernels, polar_part(): pl.pallas_call(functools.partial(polar_kernel, slots, cols), out_shape=ja...  5.31 us
    all_to_all x1, waiting for transfers between devices, body(): lax.all_to_all(outgoing, 'lon', split_axis=0, concat_axis=0, tiled=True)  5.2 us
    pallas_call x1, Pallas kernels, tile_part(): pl.pallas_call(functools.partial(tile_kernel, 32), out_shape=(jax.ShapeDt...  4.76 us
    pallas_call x1, Pallas kernels, prep(): pl.pallas_call(functools.partial(prep_kernel, slots), out_shape=(jax.Shap...  4.29 us
    all_to_all x1, starting transfers between devices, body(): lax.all_to_all(outgoing, 'lon', split_axis=0, concat_axis=0, tiled=True)  3.73 us
  transfers between devices with their start and end apart: 3, of which 2 were waited for; matrix products, arithmetic and copies ran while one was open for 0% of the time, Pallas kernels for 13%

profile of v1, /device:TPU:0, one launch (start us, length us, event | category | flops | bytes accessed | tf_op | source)
XLA Modules:
  0.0 35.7 jit_solution(3711544400634195133)
XLA Ops:
  0.6 4.3 %prep.1 = (bf16[64,32,128]{2,1,0:T(8,128)(2,1)}, bf16[16,144,128]{2,1,0:T(8,128)(2,1)}) custom-call(s32[32]{0:T(128)} %rows_ref.1, s32[32]{0:T(128)} %owner_ref.1, bf16[64,32,128]{2,1,0:T(8,128)(2,1)} %field_hbm.1, s32[32,64]{1,0:T(8,128)} %bitcast.2), custom_call_target="tpu_custom_call" | custom-call | flops 1000000 | bytes 2000000 | tf_op jit(solution)/shard_map/prep/pallas_call | solution.py:112
  4.9 0.5 %collective-permute-start.1 = (bf16[64,32,128]{2,1,0:T(8,128)(2,1)}, bf16[64,32,128]{2,1,0:T(8,128)(2,1)S(1)}, u32[]{:S(2)}, u32[]{:S(2)}) collective-permute-start(bf16[64,32,128]{2,1,0:T(8,128)(2,1)} %get-tuple-element.7.own_ref), channel_id=1, source_target_pairs={{0,1},{1,0},{2,3},{3,2},{4,5},{5,4},{6,7},{7,6},{8,9},{9,8},{10,11... | collective-permute-start | bytes 1572872 | tf_op jit(solution)/shard_map/ppermute | solution.py:278
  5.4 5.7 %collective-permute-start = (bf16[64,32,128]{2,1,0:T(8,128)(2,1)}, bf16[64,32,128]{2,1,0:T(8,128)(2,1)S(1)}, u32[]{:S(2)}, u32[]{:S(2)}) collective-permute-start(bf16[64,32,128]{2,1,0:T(8,128)(2,1)} %get-tuple-element.7.own_ref), channel_id=1, source_target_pairs={{0,15},{1,2},{2,1},{3,4},{4,3},{5,6},{6,5},{7,8},{8,7},{9,10},{10,... | collective-permute-start | bytes 1572872 | tf_op jit(solution)/shard_map/ppermute | solution.py:277
  11.1 0.0 copy-start
  11.1 0.0 copy-start.1
  11.1 0.0 copy-start.2
  11.1 0.0 copy-start.3
  11.1 0.0 copy-start.4
  11.1 3.7 %all-to-all-start = ((bf16[16,144,128]{2,1,0:T(8,128)(2,1)}), bf16[16,144,128]{2,1,0:T(8,128)(2,1)S(1)}, u32[]{:S(2)}, u32[]{:S(2)}) async-start(bf16[16,144,128]{2,1,0:T(8,128)(2,1)} %get-tuple-element.9), calls=%async_computation | async-start | bytes 1179648 | tf_op jit(solution)/shard_map/all_to_all | solution.py:279
  14.9 0.0 copy-start.5
  14.9 0.0 copy-start.6
  14.9 0.0 collective-permute-done.1.swap_ref
  14.9 5.5 %collective-permute-done.cross_ref = bf16[64,32,128]{2,1,0:T(8,128)(2,1)S(1)} collective-permute-done((bf16[64,32,128]{2,1,0:T(8,128)(2,1)}, bf16[64,32,128]{2,1,0:T(8,128)(2,1)S(1)}, u32[]{:S(2)}, u32[]{:S(2)}) %collective-permute-start) | collective-permute-done | bytes 524320 | tf_op jit(solution)/shard_map/ppermute | solution.py:277
  20.4 0.0 copy-done
  20.4 0.0 copy-done.1
  20.4 0.0 copy-done.2
  20.4 0.0 copy-done.3
  20.4 0.0 copy-done.4
  20.4 0.0 copy-done.5
  20.4 0.0 copy-done.6
  20.4 4.8 %tile.1 = (bf16[64,32,128]{2,1,0:T(8,128)(2,1)}, bf16[128,160]{1,0:T(8,128)(2,1)S(1)}, bf16[128,160]{1,0:T(8,128)(2,1)S(1)}) custom-call(f32[31]{0:T(128)S(1)} %copy-done.5, bf16[64,32,128]{2,1,0:T(8,128)(2,1)S(1)} %copy-done.1, bf16[64,32,128]{2,1,0:T(8,128)(2,1)S(1)} %collective-permute-done.cross_ref, ...), custom_call_target="tpu_custom_call" | custom-call | flops 49999998976 | bytes 3000000 | tf_op jit(solution)/shard_map/tile/pallas_call | solution.py:184
  25.2 5.2 %all-to-all-done.recv_ref = bf16[16,144,128]{2,1,0:T(8,128)(2,1)S(1)} async-done(((bf16[16,144,128]{2,1,0:T(8,128)(2,1)}), bf16[16,144,128]{2,1,0:T(8,128)(2,1)S(1)}, u32[]{:S(2)}, u32[]{:S(2)}) %all-to-all-start) | async-done | bytes 589856 | tf_op jit(solution)/shard_map/all_to_all | solution.py:279
  30.4 5.3 %polar.1 = bf16[4,512,128]{2,1,0:T(8,128)(2,1)} custom-call(bf16[16,144,128]{2,1,0:T(8,128)(2,1)S(1)} %all-to-all-done.recv_ref, bf16[128,160]{1,0:T(8,128)(2,1)S(1)} %get-tuple-element.10.high_ref, bf16[128,160]{1,0:T(8,128)(2,1)S(1)} %get-tuple-element.11.low_ref, f32[15,128]{1,0:T(8,128)S(1)} %copy-done.4, f32[1,128]{1,0:T(1,128)S(1)} %bitcast.5, ...), custom_call_target="tpu_custom_call" | custom-call | flops 600000000 | bytes 2000000 | tf_op jit(solution)/shard_map/polar/pallas_call | solution.py:238
Async XLA Ops:
  4.9 10.0 %collective-permute-start.1 = (bf16[64,32,128]{2,1,0:T(8,128)(2,1)}, bf16[64,32,128]{2,1,0:T(8,128)(2,1)S(1)}, u32[]{:S(2)}, u32[]{:S(2)}) collective-permute-start(bf16[64,32,128]{2,1,0:T(8,128)(2,1)} %get-tuple-element.7.own_ref), channel_id=1, source_target_pairs={{0,1},{1,0},{2,3},{3,2},{4,5},{5,4},{6,7},{7,6},{8,9},{9,8},{10,11... | collective-permute-start | bytes 1572872 | tf_op jit(solution)/shard_map/ppermute | solution.py:278
  5.4 14.9 %collective-permute-start = (bf16[64,32,128]{2,1,0:T(8,128)(2,1)}, bf16[64,32,128]{2,1,0:T(8,128)(2,1)S(1)}, u32[]{:S(2)}, u32[]{:S(2)}) collective-permute-start(bf16[64,32,128]{2,1,0:T(8,128)(2,1)} %get-tuple-element.7.own_ref), channel_id=1, source_target_pairs={{0,15},{1,2},{2,1},{3,4},{4,3},{5,6},{6,5},{7,8},{8,7},{9,10},{10,... | collective-permute-start | bytes 1572872 | tf_op jit(solution)/shard_map/ppermute | solution.py:277
  11.1 9.3 %copy-start = (s32[64,32]{0,1:T(8,128)S(1)}, s32[64,32]{0,1:T(8,128)}, u32[]{:S(2)}) copy-start(s32[64,32]{0,1:T(8,128)} %param.10) | copy-start | bytes 24580
  11.1 9.3 %copy-start.1 = (bf16[64,32,128]{2,1,0:T(8,128)(2,1)S(1)}, bf16[64,32,128]{2,1,0:T(8,128)(2,1)}, u32[]{:S(2)}) copy-start(bf16[64,32,128]{2,1,0:T(8,128)(2,1)} %get-tuple-element.7.own_ref) | copy-start | bytes 1572868
  11.1 9.3 %copy-start.2 = (bf16[128,512]{1,0:T(8,128)(2,1)S(1)}, bf16[128,512]{1,0:T(8,128)(2,1)}, u32[]{:S(2)}) copy-start(bf16[128,512]{1,0:T(8,128)(2,1)} %up_ref.3) | copy-start | bytes 393220
  11.1 9.3 %copy-start.3 = (bf16[512,128]{1,0:T(8,128)(2,1)S(1)}, bf16[512,128]{1,0:T(8,128)(2,1)}, u32[]{:S(2)}) copy-start(bf16[512,128]{1,0:T(8,128)(2,1)} %down_ref.3) | copy-start | bytes 393220
  11.1 9.3 %copy-start.4 = (f32[15,128]{1,0:T(8,128)S(1)}, f32[15,128]{1,0:T(8,128)}, u32[]{:S(2)}) copy-start(f32[15,128]{1,0:T(8,128)} %taps_ref.3) | copy-start | bytes 23044
  11.1 19.2 %all-to-all-start = ((bf16[16,144,128]{2,1,0:T(8,128)(2,1)}), bf16[16,144,128]{2,1,0:T(8,128)(2,1)S(1)}, u32[]{:S(2)}, u32[]{:S(2)}) async-start(bf16[16,144,128]{2,1,0:T(8,128)(2,1)} %get-tuple-element.9), calls=%async_computation | async-start | bytes 1179648 | tf_op jit(solution)/shard_map/all_to_all | solution.py:279
  14.9 5.5 %copy-start.5 = (f32[31]{0:T(128)S(1)}, f32[31]{0:T(128)}, u32[]{:S(2)}) copy-start(f32[31]{0:T(128)} %polar_taps_ref.1) | copy-start | bytes 376
  14.9 5.5 %copy-start.6 = (f32[128]{0:T(128)S(1)}, f32[128]{0:T(128)}, u32[]{:S(2)}) copy-start(f32[128]{0:T(128)} %param.12) | copy-start | bytes 1540

commit v2 on v1

--- a/solution.py
+++ b/solution.py
@@ -9,6 +9,8 @@
 
 DILATION_STEP = 4
 EXTRA = 16
+PARTS = 1
+SHARES = 2
 VMEM_BYTES = 48 * 1024 * 1024
 F32 = jnp.float32
 BF16 = jnp.bfloat16
@@ -53,38 +55,44 @@
 
 
 def prep_kernel(
-    slots, rows_ref, owner_ref, field_hbm, mask_ref, masked_ref, out_hbm,
-    count, field, mask_f, extra, extra_half, load_sems, row_sems, extra_sem,
+    slots, rows_hbm, owner_hbm, field_hbm, mask_hbm, masked_hbm, out_hbm,
+    rows, owners, count, field, masked, mask_t, mask_f, extra, extra_half, small_sems, load_sems, store_sems, row_sems, extra_sem,
 ):
     lat_rows, cols, channels = field.shape
     tiles = out_hbm.shape[0]
     parts = load_sems.shape[0]
     some = lat_rows // parts
-    entries = owner_ref.shape[0]
-    loads = [
-        pltpu.make_async_copy(field_hbm.at[pl.ds(p * some, some)], field.at[pl.ds(p * some, some)], load_sems.at[p])
-        for p in range(parts)
+    entries = owners.shape[0]
+    small = [
+        pltpu.make_async_copy(rows_hbm, rows, small_sems.at[0]),
+        pltpu.make_async_copy(owner_hbm, owners, small_sems.at[1]),
+        pltpu.make_async_copy(mask_hbm, mask_t, small_sems.at[2]),
     ]
-    for load in loads:
-        load.start()
-    mask = mask_ref[...].astype(F32).T
+    blocks = [pl.ds(p * some, some) for p in range(parts)]
+    loads = [pltpu.make_async_copy(field_hbm.at[b], field.at[b], load_sems.at[p]) for p, b in enumerate(blocks)]
+    stores = [pltpu.make_async_copy(masked.at[b], masked_hbm.at[b], store_sems.at[p]) for p, b in enumerate(blocks)]
+    for copy in small + loads:
+        copy.start()
     mask_f[...] = jnp.zeros_like(mask_f)
-    mask_f[:, :cols] = mask
     extra[...] = jnp.zeros_like(extra)
     for tile in range(tiles):
         count[tile] = 0
 
     def row_copy(e, row, owner, rank):
         return pltpu.make_async_copy(
-            masked_ref.at[row],
+            masked.at[row],
             out_hbm.at[owner, pl.ds(pl.multiple_of(rank * cols, cols), cols)],
             row_sems.at[e],
         )
 
+    for copy in small:
+        copy.wait()
+    mask = mask_t[...].astype(F32).T
+    mask_f[:, :cols] = mask
     places = []
     for e in range(entries):
-        owner = owner_ref[e]
-        row = rows_ref[e]
+        owner = owners[e]
+        row = rows[e]
         rank = count[owner]
         count[owner] = rank + 1
         extra[pl.ds(owner * EXTRA + rank, 1), :] = mask_f[pl.ds(row, 1), :]
@@ -92,22 +100,23 @@
     extra_half[...] = extra[...].astype(BF16).reshape(tiles, EXTRA, channels)
     extra_copy = pltpu.make_async_copy(extra_half, out_hbm.at[:, pl.ds(slots * cols, EXTRA)], extra_sem)
     extra_copy.start()
-    for p, load in enumerate(loads):
+    for p in range(parts):
         at = slice(p * some, (p + 1) * some)
         wide = spread_mask(mask[at], channels).astype(BF16)
-        load.wait()
-        masked_ref[at] = field[at] * wide.reshape(some, cols, channels)
+        loads[p].wait()
+        masked[at] = field[at] * wide.reshape(some, cols, channels)
+        stores[p].start()
     for e, place in enumerate(places):
         row_copy(e, *place).start()
     for e, place in enumerate(places):
         row_copy(e, *place).wait()
     extra_copy.wait()
+    for store in stores:
+        store.wait()
 
 
 def prep(field, land_mask, polar_rows, polar_owner, tiles, slots):
     lat_rows, cols, channels = field.shape
-    smem = pl.BlockSpec(memory_space=pltpu.SMEM)
-    vmem = pl.BlockSpec(memory_space=pltpu.VMEM)
     hbm = pl.BlockSpec(memory_space=pltpu.HBM)
     return pl.pallas_call(
         functools.partial(prep_kernel, slots),
@@ -115,15 +124,21 @@
             jax.ShapeDtypeStruct(field.shape, BF16),
             jax.ShapeDtypeStruct((tiles, slots * cols + EXTRA, channels), BF16),
         ),
-        in_specs=[smem, smem, hbm, vmem],
-        out_specs=(vmem, hbm),
+        in_specs=[hbm] * 4,
+        out_specs=(hbm, hbm),
         scratch_shapes=[
+            pltpu.SMEM(polar_rows.shape, jnp.int32),
+            pltpu.SMEM(polar_owner.shape, jnp.int32),
             pltpu.SMEM((tiles,), jnp.int32),
             pltpu.VMEM(field.shape, BF16),
+            pltpu.VMEM(field.shape, BF16),
+            pltpu.VMEM((cols, lat_rows), jnp.int32),
             pltpu.VMEM((lat_rows, channels), F32),
             pltpu.VMEM((tiles * EXTRA, channels), F32),
             pltpu.VMEM((tiles, EXTRA, channels), BF16),
-            pltpu.SemaphoreType.DMA((4,)),
+            pltpu.SemaphoreType.DMA((3,)),
+            pltpu.SemaphoreType.DMA((PARTS,)),
+            pltpu.SemaphoreType.DMA((PARTS,)),
             pltpu.SemaphoreType.DMA(polar_owner.shape),
             pltpu.SemaphoreType.DMA,
         ],
@@ -134,7 +149,7 @@
 
 def tile_kernel(
     chunk, polar_taps_ref, own_ref, cross_ref, swap_ref, mask_ref, taps_ref, gain_ref, up_ref, down_ref,
-    mixed_ref, high_ref, low_ref, left, right, mask_f,
+    mixed_ref, bands_ref, left, right, mask_f,
 ):
     lat_rows, cols, channels = own_ref.shape
     me = lax.axis_index("lon")
@@ -165,7 +180,7 @@
 
     lax.fori_loop(0, lat_rows // chunk, some_rows, 0)
 
-    n, depth = high_ref.shape
+    n, depth = bands_ref.shape[0] // 2, bands_ref.shape[1]
     n_taps = polar_taps_ref.shape[0]
     offset = lax.broadcasted_iota(jnp.int32, (n, depth), 1) - lax.broadcasted_iota(jnp.int32, (n, depth), 0)
     first = (depth - n) // 2 - n_taps // 2
@@ -173,8 +188,8 @@
     for k in range(n_taps):
         band = jnp.where(offset == k + first, polar_taps_ref[k], band)
     high = band.astype(BF16)
-    high_ref[...] = high
-    low_ref[...] = (band - high.astype(F32)).astype(BF16)
+    bands_ref[:n] = high
+    bands_ref[n:] = (band - high.astype(F32)).astype(BF16)
 
 
 def tile_part(polar_taps, masked, cross, swap, land_mask, weights):
@@ -185,11 +200,10 @@
         functools.partial(tile_kernel, 32),
         out_shape=(
             jax.ShapeDtypeStruct(masked.shape, BF16),
-            jax.ShapeDtypeStruct((128, 160), BF16),
-            jax.ShapeDtypeStruct((128, 160), BF16),
+            jax.ShapeDtypeStruct((256, 160), BF16),
         ),
         in_specs=[smem] + [vmem] * 8,
-        out_specs=(vmem, vmem, vmem),
+        out_specs=(vmem, vmem),
         scratch_shapes=[pltpu.VMEM(masked.shape, BF16)] * 2 + [pltpu.VMEM((lat_rows, cols), F32)],
         compiler_params=pltpu.CompilerParams(vmem_limit_bytes=VMEM_BYTES),
         cost_estimate=pl.CostEstimate(flops=5 * 10**10, bytes_accessed=3 * 10**6, transcendentals=10**6),
@@ -198,57 +212,61 @@
 
 
 def polar_kernel(
-    slots, cols, recv_ref, high_ref, low_ref, taps_ref, gain_ref, up_ref, down_ref,
+    slots, cols, recv_ref, bands_ref, taps_ref, gain_ref, up_ref, down_ref,
     out_hbm, circle, out, sems,
 ):
     tiles, _, channels = recv_ref.shape
-    n, depth = high_ref.shape
+    n, depth = bands_ref.shape[0] // 2, bands_ref.shape[1]
     pad = (depth - n) // 2
     nlon = tiles * cols
     taps = [taps_ref[k : k + 1] for k in range(taps_ref.shape[0])]
     extra = recv_ref[:, slots * cols :, :].astype(F32)
     copies = []
-    for slot in range(slots):
-        wide = spread_mask(extra[:, slot, :cols], channels)
-        recv = jnp.concatenate([recv_ref[t, slot * cols : (slot + 1) * cols, :] for t in range(tiles)], axis=0)
-        own = jnp.where(wide > 0.5, recv.astype(F32), 0.0)
-        pieces = [own[t * cols : (t + 1) * cols] for t in range(tiles)]
-        triples = [(pieces[t - 1], pieces[t], pieces[(t + 1) % tiles]) for t in range(tiles)]
-        branch = branch_rows(triples, taps, gain_ref[...], up_ref[...], down_ref[...])
-        mixed = (wide * (own + branch.astype(BF16).astype(F32))).astype(BF16)
-        circle[slot, pad : nlon + pad, :] = mixed
-        circle[slot, :pad, :] = mixed[nlon - pad :]
-        circle[slot, nlon + pad :, :] = mixed[:pad]
+    share = nlon // n // SHARES
+    for pair in range(slots // 2):
+        for half in range(2):
+            slot = pair * 2 + half
+            pieces = [recv_ref[t, slot * cols : (slot + 1) * cols, :].astype(F32) for t in range(tiles)]
+            triples = [(pieces[t - 1], pieces[t], pieces[(t + 1) % tiles]) for t in range(tiles)]
+            branch = branch_rows(triples, taps, gain_ref[...], up_ref[...], down_ref[...])
+            wide = spread_mask(extra[:, slot, :cols], channels)
+            own = jnp.concatenate(pieces, axis=0)
+            mixed = jnp.where(wide > 0.5, own + branch.astype(BF16).astype(F32), 0.0).astype(BF16)
+            lanes = slice(half * channels, (half + 1) * channels)
+            circle[pair, pad : nlon + pad, lanes] = mixed
+            circle[pair, :pad, lanes] = mixed[nlon - pad :]
+            circle[pair, nlon + pad :, lanes] = mixed[:pad]
         for b in range(nlon // n):
-            window = circle[slot, b * n : b * n + depth, :]
-            out[slot, b * n : (b + 1) * n, :] = (
-                jnp.dot(high_ref[...], window, preferred_element_type=F32)
-                + jnp.dot(low_ref[...], window, preferred_element_type=F32)
-            ).astype(BF16)
-        copies.append(pltpu.make_async_copy(out.at[slot], out_hbm.at[slot], sems.at[slot]))
-        copies[-1].start()
+            both = jnp.dot(bands_ref[...], circle[pair, b * n : b * n + depth, :], preferred_element_type=F32)
+            rows = (both[:n] + both[n:]).astype(BF16)
+            for half in range(2):
+                out[pair * 2 + half, b * n : (b + 1) * n, :] = rows[:, half * channels : (half + 1) * channels]
+            if (b + 1) % share == 0:
+                at = (pl.ds(pair * 2, 2), pl.ds((b + 1 - share) * n, share * n))
+                copies.append(pltpu.make_async_copy(out.at[at], out_hbm.at[at], sems.at[len(copies)]))
+                copies[-1].start()
     for copy in copies:
         copy.wait()
 
 
-def polar_part(recv, high, low, weights, slots, cols):
+def polar_part(recv, bands, weights, slots, cols):
     tiles, _, channels = recv.shape
     vmem = pl.BlockSpec(memory_space=pltpu.VMEM)
     shape = (slots, tiles * cols, channels)
     return pl.pallas_call(
         functools.partial(polar_kernel, slots, cols),
         out_shape=jax.ShapeDtypeStruct(shape, BF16),
-        in_specs=[vmem] * 7,
+        in_specs=[vmem] * 6,
         out_specs=pl.BlockSpec(memory_space=pltpu.HBM),
         scratch_shapes=[
-            pltpu.VMEM((slots, tiles * cols + 32, channels), BF16),
+            pltpu.VMEM((slots // 2, tiles * cols + 32, 2 * channels), BF16),
             pltpu.VMEM(shape, BF16),
-            pltpu.SemaphoreType.DMA((slots,)),
+            pltpu.SemaphoreType.DMA((slots // 2 * SHARES,)),
         ],
         compiler_params=pltpu.CompilerParams(vmem_limit_bytes=VMEM_BYTES),
         cost_estimate=pl.CostEstimate(flops=6 * 10**8, bytes_accessed=2 * 10**6, transcendentals=10**6),
         name="polar",
-    )(recv, high, low, *weights)
+    )(recv, bands, *weights)
 
 
 def body(
@@ -277,8 +295,8 @@
     cross = lax.ppermute(masked, "lon", cross_pairs)
     swap = lax.ppermute(masked, "lon", swap_pairs)
     recv = lax.all_to_all(outgoing, "lon", split_axis=0, concat_axis=0, tiled=True)
-    mixed, high, low = tile_part(polar_taps, masked, cross, swap, land_mask, weights)
-    polar = polar_part(recv, high, low, weights, slots, cols)
+    mixed, bands = tile_part(polar_taps, masked, cross, swap, land_mask, weights)
+    polar = polar_part(recv, bands, weights, slots, cols)
     return (mixed, polar)
 
 

time: 36 us -> 32.8 us (0.911)
  Pallas kernels: 14.4 us -> 11.2 us
    pallas_call x1, Pallas kernels: 4.29 us -> 2.42 us  [prep(): pl.pallas_call(functools.partial(prep_kernel, slots), out_shape=(jax.Shap...]
    pallas_call x1, Pallas kernels: 5.31 us -> 4.01 us  [polar_part(): pl.pallas_call(functools.partial(polar_kernel, slots, cols), out_shape=ja...]
  transfers between devices with their start and end apart: 3 -> 3, of which waited for: 2 -> 2; matrix products, arithmetic and copies ran while one was open for 0% -> 0% of each run, Pallas kernels for 13% -> 15%
where the time goes in v2:
time: 32.8 us; the launch traced here: 32.5 us
  Pallas kernels  11.2 us (34%)
  waiting for transfers between devices  10.7 us (33%)
  starting transfers between devices  9.91 us (30%)
  between operations  0.71 us (2%)
    ppermute x1, starting transfers between devices, body(): cross = lax.ppermute(masked, 'lon', cross_pairs)  5.67 us
    ppermute x1, waiting for transfers between devices, body(): cross = lax.ppermute(masked, 'lon', cross_pairs)  5.47 us
    all_to_all x1, waiting for transfers between devices, body(): lax.all_to_all(outgoing, 'lon', split_axis=0, concat_axis=0, tiled=True)  5.21 us
    pallas_call x1, Pallas kernels, tile_part(): pl.pallas_call(functools.partial(tile_kernel, 32), out_shape=(jax.ShapeDt...  4.74 us
    pallas_call x1, Pallas kernels, polar_part(): pl.pallas_call(functools.partial(polar_kernel, slots, cols), out_shape=ja...  4.01 us
    all_to_all x1, starting transfers between devices, body(): lax.all_to_all(outgoing, 'lon', split_axis=0, concat_axis=0, tiled=True)  3.73 us
    pallas_call x1, Pallas kernels, prep(): pl.pallas_call(functools.partial(prep_kernel, slots), out_shape=(jax.Shap...  2.42 us
  transfers between devices with their start and end apart: 3, of which 2 were waited for; matrix products, arithmetic and copies ran while one was open for 0% of the time, Pallas kernels for 15%

profile of v2, /device:TPU:0, one launch (start us, length us, event | category | flops | bytes accessed | tf_op | source)
XLA Modules:
  0.0 32.5 jit_solution(14718598260160899058)
XLA Ops:
  0.6 2.4 %prep.1 = (bf16[64,32,128]{2,1,0:T(8,128)(2,1)}, bf16[16,144,128]{2,1,0:T(8,128)(2,1)}) custom-call(s32[32]{0:T(128)} %rows_hbm.1, s32[32]{0:T(128)} %owner_hbm.1, bf16[64,32,128]{2,1,0:T(8,128)(2,1)} %field_hbm.1, s32[32,64]{1,0:T(8,128)} %bitcast.2), custom_call_target="tpu_custom_call" | custom-call | flops 1000000 | bytes 2000000 | tf_op jit(solution)/shard_map/prep/pallas_call | solution.py:121
  3.1 0.5 %collective-permute-start.1 = (bf16[64,32,128]{2,1,0:T(8,128)(2,1)}, bf16[64,32,128]{2,1,0:T(8,128)(2,1)S(1)}, u32[]{:S(2)}, u32[]{:S(2)}) collective-permute-start(bf16[64,32,128]{2,1,0:T(8,128)(2,1)} %get-tuple-element.6.own_ref), channel_id=1, source_target_pairs={{0,1},{1,0},{2,3},{3,2},{4,5},{5,4},{6,7},{7,6},{8,9},{9,8},{10,11... | collective-permute-start | bytes 1572872 | tf_op jit(solution)/shard_map/ppermute | solution.py:296
  3.6 5.7 %collective-permute-start = (bf16[64,32,128]{2,1,0:T(8,128)(2,1)}, bf16[64,32,128]{2,1,0:T(8,128)(2,1)S(1)}, u32[]{:S(2)}, u32[]{:S(2)}) collective-permute-start(bf16[64,32,128]{2,1,0:T(8,128)(2,1)} %get-tuple-element.6.own_ref), channel_id=1, source_target_pairs={{0,15},{1,2},{2,1},{3,4},{4,3},{5,6},{6,5},{7,8},{8,7},{9,10},{10,... | collective-permute-start | bytes 1572872 | tf_op jit(solution)/shard_map/ppermute | solution.py:295
  9.2 0.0 copy-start
  9.2 0.0 copy-start.1
  9.2 0.0 copy-start.2
  9.2 0.0 copy-start.3
  9.2 0.0 copy-start.4
  9.3 3.7 %all-to-all-start = ((bf16[16,144,128]{2,1,0:T(8,128)(2,1)}), bf16[16,144,128]{2,1,0:T(8,128)(2,1)S(1)}, u32[]{:S(2)}, u32[]{:S(2)}) async-start(bf16[16,144,128]{2,1,0:T(8,128)(2,1)} %get-tuple-element.8), calls=%async_computation | async-start | bytes 1179648 | tf_op jit(solution)/shard_map/all_to_all | solution.py:297
  13.0 0.0 copy-start.5
  13.0 0.0 copy-start.6
  13.0 0.0 collective-permute-done.1.swap_ref
  13.0 5.5 %collective-permute-done.cross_ref = bf16[64,32,128]{2,1,0:T(8,128)(2,1)S(1)} collective-permute-done((bf16[64,32,128]{2,1,0:T(8,128)(2,1)}, bf16[64,32,128]{2,1,0:T(8,128)(2,1)S(1)}, u32[]{:S(2)}, u32[]{:S(2)}) %collective-permute-start) | collective-permute-done | bytes 524320 | tf_op jit(solution)/shard_map/ppermute | solution.py:295
  18.5 0.0 copy-done
  18.5 0.0 copy-done.1
  18.5 0.0 copy-done.2
  18.5 0.0 copy-done.3
  18.5 0.0 copy-done.4
  18.5 0.0 copy-done.5
  18.5 0.0 copy-done.6
  18.5 4.7 %tile.1 = (bf16[64,32,128]{2,1,0:T(8,128)(2,1)}, bf16[256,160]{1,0:T(8,128)(2,1)S(1)}) custom-call(f32[31]{0:T(128)S(1)} %copy-done.5, bf16[64,32,128]{2,1,0:T(8,128)(2,1)S(1)} %copy-done.1, bf16[64,32,128]{2,1,0:T(8,128)(2,1)S(1)} %collective-permute-done.cross_ref, bf16[64,32,128]{2,1,0:T(8,128)(2,1)S(1)} %collective-permute-done.1.swap_ref, ...), custom_call_target="tpu_custom_call" | custom-call | flops 49999998976 | bytes 3000000 | tf_op jit(solution)/shard_map/tile/pallas_call | solution.py:199
  23.3 5.2 %all-to-all-done.recv_ref = bf16[16,144,128]{2,1,0:T(8,128)(2,1)S(1)} async-done(((bf16[16,144,128]{2,1,0:T(8,128)(2,1)}), bf16[16,144,128]{2,1,0:T(8,128)(2,1)S(1)}, u32[]{:S(2)}, u32[]{:S(2)}) %all-to-all-start) | async-done | bytes 589856 | tf_op jit(solution)/shard_map/all_to_all | solution.py:297
  28.5 4.0 %polar.1 = bf16[4,512,128]{2,1,0:T(8,128)(2,1)} custom-call(bf16[16,144,128]{2,1,0:T(8,128)(2,1)S(1)} %all-to-all-done.recv_ref, bf16[256,160]{1,0:T(8,128)(2,1)S(1)} %get-tuple-element.9.bands_ref, f32[15,128]{1,0:T(8,128)S(1)} %copy-done.4, f32[1,128]{1,0:T(1,128)S(1)} %bitcast.5, bf16[128,512]{1,0:T(8,128)(2,1)S(1)} %copy-done.2, ...), custom_call_target="tpu_custom_call" | custom-call | flops 600000000 | bytes 2000000 | tf_op jit(solution)/shard_map/polar/pallas_call | solution.py:256
Async XLA Ops:
  3.1 10.0 %collective-permute-start.1 = (bf16[64,32,128]{2,1,0:T(8,128)(2,1)}, bf16[64,32,128]{2,1,0:T(8,128)(2,1)S(1)}, u32[]{:S(2)}, u32[]{:S(2)}) collective-permute-start(bf16[64,32,128]{2,1,0:T(8,128)(2,1)} %get-tuple-element.6.own_ref), channel_id=1, source_target_pairs={{0,1},{1,0},{2,3},{3,2},{4,5},{5,4},{6,7},{7,6},{8,9},{9,8},{10,11... | collective-permute-start | bytes 1572872 | tf_op jit(solution)/shard_map/ppermute | solution.py:296
  3.6 14.9 %collective-permute-start = (bf16[64,32,128]{2,1,0:T(8,128)(2,1)}, bf16[64,32,128]{2,1,0:T(8,128)(2,1)S(1)}, u32[]{:S(2)}, u32[]{:S(2)}) collective-permute-start(bf16[64,32,128]{2,1,0:T(8,128)(2,1)} %get-tuple-element.6.own_ref), channel_id=1, source_target_pairs={{0,15},{1,2},{2,1},{3,4},{4,3},{5,6},{6,5},{7,8},{8,7},{9,10},{10,... | collective-permute-start | bytes 1572872 | tf_op jit(solution)/shard_map/ppermute | solution.py:295
  9.2 9.3 %copy-start = (s32[64,32]{0,1:T(8,128)S(1)}, s32[64,32]{0,1:T(8,128)}, u32[]{:S(2)}) copy-start(s32[64,32]{0,1:T(8,128)} %param.10) | copy-start | bytes 24580
  9.2 9.3 %copy-start.1 = (bf16[64,32,128]{2,1,0:T(8,128)(2,1)S(1)}, bf16[64,32,128]{2,1,0:T(8,128)(2,1)}, u32[]{:S(2)}) copy-start(bf16[64,32,128]{2,1,0:T(8,128)(2,1)} %get-tuple-element.6.own_ref) | copy-start | bytes 1572868
  9.2 9.3 %copy-start.2 = (bf16[128,512]{1,0:T(8,128)(2,1)S(1)}, bf16[128,512]{1,0:T(8,128)(2,1)}, u32[]{:S(2)}) copy-start(bf16[128,512]{1,0:T(8,128)(2,1)} %up_ref.3) | copy-start | bytes 393220
  9.2 9.3 %copy-start.3 = (bf16[512,128]{1,0:T(8,128)(2,1)S(1)}, bf16[512,128]{1,0:T(8,128)(2,1)}, u32[]{:S(2)}) copy-start(bf16[512,128]{1,0:T(8,128)(2,1)} %down_ref.3) | copy-start | bytes 393220
  9.2 9.3 %copy-start.4 = (f32[15,128]{1,0:T(8,128)S(1)}, f32[15,128]{1,0:T(8,128)}, u32[]{:S(2)}) copy-start(f32[15,128]{1,0:T(8,128)} %taps_ref.3) | copy-start | bytes 23044
  9.3 19.2 %all-to-all-start = ((bf16[16,144,128]{2,1,0:T(8,128)(2,1)}), bf16[16,144,128]{2,1,0:T(8,128)(2,1)S(1)}, u32[]{:S(2)}, u32[]{:S(2)}) async-start(bf16[16,144,128]{2,1,0:T(8,128)(2,1)} %get-tuple-element.8), calls=%async_computation | async-start | bytes 1179648 | tf_op jit(solution)/shard_map/all_to_all | solution.py:297
  13.0 5.5 %copy-start.5 = (f32[31]{0:T(128)S(1)}, f32[31]{0:T(128)}, u32[]{:S(2)}) copy-start(f32[31]{0:T(128)} %polar_taps_ref.1) | copy-start | bytes 376
  13.0 5.5 %copy-start.6 = (f32[128]{0:T(128)S(1)}, f32[128]{0:T(128)}, u32[]{:S(2)}) copy-start(f32[128]{0:T(128)} %param.12) | copy-start | bytes 1540

commit v3 on v2

--- a/solution.py
+++ b/solution.py
@@ -8,7 +8,8 @@
 from jax.sharding import PartitionSpec as P
 
 DILATION_STEP = 4
-EXTRA = 16
+EXTRA = 8
+TILE_FLOPS = 7 * 10**9
 PARTS = 1
 SHARES = 2
 VMEM_BYTES = 48 * 1024 * 1024
@@ -148,21 +149,23 @@
 
 
 def tile_kernel(
-    chunk, polar_taps_ref, own_ref, cross_ref, swap_ref, mask_ref, taps_ref, gain_ref, up_ref, down_ref,
+    chunk, polar_taps_ref, own_ref, cross_ref, upper_ref, lower_ref, mask_ref, taps_ref, gain_ref, up_ref, down_ref,
     mixed_ref, bands_ref, left, right, mask_f,
 ):
     lat_rows, cols, channels = own_ref.shape
-    me = lax.axis_index("lon")
-    odd = lax.rem(me, 2)
+    half = lat_rows // 2
+    odd = lax.rem(lax.axis_index("lon"), 2)
 
     @pl.when(odd == 0)
     def _():
         left[...] = cross_ref[...]
-        right[...] = swap_ref[...]
+        right[:half] = upper_ref[...]
+        right[half:] = lower_ref[...]
 
     @pl.when(odd == 1)
     def _():
-        left[...] = swap_ref[...]
+        left[:half] = upper_ref[...]
+        left[half:] = lower_ref[...]
         right[...] = cross_ref[...]
 
     mask_f[...] = mask_ref[...].astype(F32).T
@@ -192,7 +195,7 @@
     bands_ref[n:] = (band - high.astype(F32)).astype(BF16)
 
 
-def tile_part(polar_taps, masked, cross, swap, land_mask, weights):
+def tile_part(polar_taps, masked, cross, swaps, land_mask, weights):
     lat_rows, cols, channels = masked.shape
     smem = pl.BlockSpec(memory_space=pltpu.SMEM)
     vmem = pl.BlockSpec(memory_space=pltpu.VMEM)
@@ -202,13 +205,13 @@
             jax.ShapeDtypeStruct(masked.shape, BF16),
             jax.ShapeDtypeStruct((256, 160), BF16),
         ),
-        in_specs=[smem] + [vmem] * 8,
+        in_specs=[smem] + [vmem] * 9,
         out_specs=(vmem, vmem),
         scratch_shapes=[pltpu.VMEM(masked.shape, BF16)] * 2 + [pltpu.VMEM((lat_rows, cols), F32)],
         compiler_params=pltpu.CompilerParams(vmem_limit_bytes=VMEM_BYTES),
-        cost_estimate=pl.CostEstimate(flops=5 * 10**10, bytes_accessed=3 * 10**6, transcendentals=10**6),
+        cost_estimate=pl.CostEstimate(flops=TILE_FLOPS, bytes_accessed=3 * 10**6, transcendentals=10**6),
         name="tile",
-    )(polar_taps, masked, cross, swap, land_mask.T, *weights)
+    )(polar_taps, masked, cross, *swaps, land_mask.T, *weights)
 
 
 def polar_kernel(
@@ -293,9 +296,10 @@
     swap_pairs = [(i, i ^ 1) for i in range(tiles)]
     cross_pairs = [(i, (i + 1) % tiles if i % 2 else (i - 1) % tiles) for i in range(tiles)]
     cross = lax.ppermute(masked, "lon", cross_pairs)
-    swap = lax.ppermute(masked, "lon", swap_pairs)
+    half = lat_rows // 2
+    swaps = [lax.ppermute(masked[:half], "lon", swap_pairs), lax.ppermute(masked[half:], "lon", swap_pairs)]
     recv = lax.all_to_all(outgoing, "lon", split_axis=0, concat_axis=0, tiled=True)
-    mixed, bands = tile_part(polar_taps, masked, cross, swap, land_mask, weights)
+    mixed, bands = tile_part(polar_taps, masked, cross, swaps, land_mask, weights)
     polar = polar_part(recv, bands, weights, slots, cols)
     return (mixed, polar)
 

time: 32.8 us -> 31.5 us (0.960)
  waiting for transfers between devices: 10.7 us -> 9.52 us
    ppermute x1, waiting for transfers between devices: 5.47 us -> 3.5 us  [body(): cross = lax.ppermute(masked, 'lon', cross_pairs)]
    ppermute x1 -> x2, waiting for transfers between devices: 0.01 us -> 1.39 us  [the longest x1 1.02 us: body(): lax.ppermute(masked[half:], 'lon', swap_pairs)]
    all_to_all x1, waiting for transfers between devices: 5.21 us -> 4.62 us  [body(): lax.all_to_all(outgoing, 'lon', split_axis=0, concat_axis=0, tiled=True)]
  transfers between devices with their start and end apart: 3 -> 4, of which waited for: 2 -> 4; matrix products, arithmetic and copies ran while one was open for 0% -> 0% of each run, Pallas kernels for 15% -> 15%
where the time goes in v3:
time: 31.5 us; the launch traced here: 31.2 us
  Pallas kernels  11.1 us (35%)
  starting transfers between devices  9.79 us (31%)
  waiting for transfers between devices  9.52 us (30%)
  between operations  0.72 us (2%)
    ppermute x1, starting transfers between devices, body(): cross = lax.ppermute(masked, 'lon', cross_pairs)  5.51 us
    pallas_call x1, Pallas kernels, tile_part(): pl.pallas_call(functools.partial(tile_kernel, 32), out_shape=(jax.ShapeDt...  4.74 us
    all_to_all x1, waiting for transfers between devices, body(): lax.all_to_all(outgoing, 'lon', split_axis=0, concat_axis=0, tiled=True)  4.62 us
    pallas_call x1, Pallas kernels, polar_part(): pl.pallas_call(functools.partial(polar_kernel, slots, cols), out_shape=ja...  3.99 us
    all_to_all x1, starting transfers between devices, body(): lax.all_to_all(outgoing, 'lon', split_axis=0, concat_axis=0, tiled=True)  3.71 us
    ppermute x1, waiting for transfers between devices, body(): cross = lax.ppermute(masked, 'lon', cross_pairs)  3.5 us
    pallas_call x1, Pallas kernels, prep(): pl.pallas_call(functools.partial(prep_kernel, slots), out_shape=(jax.Shap...  2.41 us
    ppermute x1, waiting for transfers between devices, body(): lax.ppermute(masked[half:], 'lon', swap_pairs)  1.02 us
  transfers between devices with their start and end apart: 4, of which 4 were waited for; matrix products, arithmetic and copies ran while one was open for 0% of the time, Pallas kernels for 15%

profile of v3, /device:TPU:0, one launch (start us, length us, event | category | flops | bytes accessed | tf_op | source)
XLA Modules:
  0.0 31.2 jit_solution(17187851955273889359)
XLA Ops:
  0.6 2.4 %prep.1 = (bf16[64,32,128]{2,1,0:T(8,128)(2,1)}, bf16[16,136,128]{2,1,0:T(8,128)(2,1)}) custom-call(s32[32]{0:T(128)} %rows_hbm.1, s32[32]{0:T(128)} %owner_hbm.1, bf16[64,32,128]{2,1,0:T(8,128)(2,1)} %field_hbm.1, s32[32,64]{1,0:T(8,128)} %bitcast.2), custom_call_target="tpu_custom_call" | custom-call | flops 1000000 | bytes 2000000 | tf_op jit(solution)/shard_map/prep/pallas_call | solution.py:122
  3.0 5.5 %collective-permute-start = (bf16[64,32,128]{2,1,0:T(8,128)(2,1)}, bf16[64,32,128]{2,1,0:T(8,128)(2,1)S(1)}, u32[]{:S(2)}, u32[]{:S(2)}) collective-permute-start(bf16[64,32,128]{2,1,0:T(8,128)(2,1)} %get-tuple-element.6.own_ref), channel_id=1, source_target_pairs={{0,15},{1,2},{2,1},{3,4},{4,3},{5,6},{6,5},{7,8},{8,7},{9,10},{10,... | collective-permute-start | bytes 1572872 | tf_op jit(solution)/shard_map/ppermute | solution.py:298
  8.6 0.0 copy-start
  8.6 3.7 %all-to-all-start = ((bf16[16,136,128]{2,1,0:T(8,128)(2,1)}), bf16[16,136,128]{2,1,0:T(8,128)(2,1)S(1)}, u32[]{:S(2)}, u32[]{:S(2)}) async-start(bf16[16,136,128]{2,1,0:T(8,128)(2,1)} %get-tuple-element.8), calls=%async_computation | async-start | bytes 1114112 | tf_op jit(solution)/shard_map/all_to_all | solution.py:301
  12.3 0.0 copy-done
  12.3 0.0 copy-start.1
  12.3 0.0 copy-start.2
  12.3 0.0 copy-start.3
  12.3 0.0 copy-start.4
  12.4 0.4 %collective-permute-start.2 = (bf16[32,32,128]{2,1,0:T(8,128)(2,1)S(1)}, bf16[32,32,128]{2,1,0:T(8,128)(2,1)S(1)}, u32[]{:S(2)}, u32[]{:S(2)}) collective-permute-start(bf16[32,32,128]{2,1,0:T(8,128)(2,1)S(1)} %get-tuple-element.10), channel_id=1, source_target_pairs={{0,1},{1,0},{2,3},{3,2},{4,5},{5,4},{6,7},{7,6},{8,9},{9,8},{10,11... | collective-permute-start | bytes 786440 | tf_op jit(solution)/shard_map/ppermute | solution.py:300
  12.7 0.0 copy-start.5
  12.7 0.0 copy-start.6
  12.7 0.2 collective-permute-start.1
  13.0 1.0 %collective-permute-done.2.lower_ref = bf16[32,32,128]{2,1,0:T(8,128)(2,1)S(1)} collective-permute-done((bf16[32,32,128]{2,1,0:T(8,128)(2,1)S(1)}, bf16[32,32,128]{2,1,0:T(8,128)(2,1)S(1)}, u32[]{:S(2)}, u32[]{:S(2)}) %collective-permute-start.2) | collective-permute-done | bytes 262176 | tf_op jit(solution)/shard_map/ppermute | solution.py:300
  14.0 0.4 %collective-permute-done.1.upper_ref = bf16[32,32,128]{2,1,0:T(8,128)(2,1)S(1)} collective-permute-done((bf16[32,32,128]{2,1,0:T(8,128)(2,1)S(1)}, bf16[32,32,128]{2,1,0:T(8,128)(2,1)S(1)}, u32[]{:S(2)}, u32[]{:S(2)}) %collective-permute-start.1) | collective-permute-done | bytes 262176 | tf_op jit(solution)/shard_map/ppermute | solution.py:300
  14.4 3.5 %collective-permute-done.cross_ref = bf16[64,32,128]{2,1,0:T(8,128)(2,1)S(1)} collective-permute-done((bf16[64,32,128]{2,1,0:T(8,128)(2,1)}, bf16[64,32,128]{2,1,0:T(8,128)(2,1)S(1)}, u32[]{:S(2)}, u32[]{:S(2)}) %collective-permute-start) | collective-permute-done | bytes 524320 | tf_op jit(solution)/shard_map/ppermute | solution.py:298
  17.9 0.0 copy-done.1
  17.9 0.0 copy-done.2
  17.9 0.0 copy-done.3
  17.9 0.0 copy-done.4
  17.9 0.0 copy-done.5
  17.9 0.0 copy-done.6
  17.9 4.7 %tile.1 = (bf16[64,32,128]{2,1,0:T(8,128)(2,1)}, bf16[256,160]{1,0:T(8,128)(2,1)S(1)}) custom-call(f32[31]{0:T(128)S(1)} %copy-done.5, bf16[64,32,128]{2,1,0:T(8,128)(2,1)S(1)} %copy-done, bf16[64,32,128]{2,1,0:T(8,128)(2,1)S(1)} %collective-permute-done.cross_ref, bf16[32,32,128]{2,1,0:T(8,128)(2,1)S(1)} %collective-permute-done.1.upper_ref, ...), custom_call_target="tpu_custom_call" | custom-call | flops 7000000000 | bytes 3000000 | tf_op jit(solution)/shard_map/tile/pallas_call | solution.py:202
  22.6 4.6 %all-to-all-done.recv_ref = bf16[16,136,128]{2,1,0:T(8,128)(2,1)S(1)} async-done(((bf16[16,136,128]{2,1,0:T(8,128)(2,1)}), bf16[16,136,128]{2,1,0:T(8,128)(2,1)S(1)}, u32[]{:S(2)}, u32[]{:S(2)}) %all-to-all-start) | async-done | bytes 557088 | tf_op jit(solution)/shard_map/all_to_all | solution.py:301
  27.3 4.0 %polar.1 = bf16[4,512,128]{2,1,0:T(8,128)(2,1)} custom-call(bf16[16,136,128]{2,1,0:T(8,128)(2,1)S(1)} %all-to-all-done.recv_ref, bf16[256,160]{1,0:T(8,128)(2,1)S(1)} %get-tuple-element.9.bands_ref, f32[15,128]{1,0:T(8,128)S(1)} %copy-done.4, f32[1,128]{1,0:T(1,128)S(1)} %bitcast.5, bf16[128,512]{1,0:T(8,128)(2,1)S(1)} %copy-done.2, ...), custom_call_target="tpu_custom_call" | custom-call | flops 600000000 | bytes 2000000 | tf_op jit(solution)/shard_map/polar/pallas_call | solution.py:259
  (1 shorter events, 0.0 us)
Async XLA Ops:
  3.0 14.8 %collective-permute-start = (bf16[64,32,128]{2,1,0:T(8,128)(2,1)}, bf16[64,32,128]{2,1,0:T(8,128)(2,1)S(1)}, u32[]{:S(2)}, u32[]{:S(2)}) collective-permute-start(bf16[64,32,128]{2,1,0:T(8,128)(2,1)} %get-tuple-element.6.own_ref), channel_id=1, source_target_pairs={{0,15},{1,2},{2,1},{3,4},{4,3},{5,6},{6,5},{7,8},{8,7},{9,10},{10,... | collective-permute-start | bytes 1572872 | tf_op jit(solution)/shard_map/ppermute | solution.py:298
  8.6 3.7 %copy-start = (bf16[64,32,128]{2,1,0:T(8,128)(2,1)S(1)}, bf16[64,32,128]{2,1,0:T(8,128)(2,1)}, u32[]{:S(2)}) copy-start(bf16[64,32,128]{2,1,0:T(8,128)(2,1)} %get-tuple-element.6.own_ref) | copy-start | bytes 1572868
  8.6 18.7 %all-to-all-start = ((bf16[16,136,128]{2,1,0:T(8,128)(2,1)}), bf16[16,136,128]{2,1,0:T(8,128)(2,1)S(1)}, u32[]{:S(2)}, u32[]{:S(2)}) async-start(bf16[16,136,128]{2,1,0:T(8,128)(2,1)} %get-tuple-element.8), calls=%async_computation | async-start | bytes 1114112 | tf_op jit(solution)/shard_map/all_to_all | solution.py:301
  12.3 5.6 %copy-start.1 = (s32[64,32]{0,1:T(8,128)S(1)}, s32[64,32]{0,1:T(8,128)}, u32[]{:S(2)}) copy-start(s32[64,32]{0,1:T(8,128)} %param.10) | copy-start | bytes 24580
  12.3 5.6 %copy-start.2 = (bf16[128,512]{1,0:T(8,128)(2,1)S(1)}, bf16[128,512]{1,0:T(8,128)(2,1)}, u32[]{:S(2)}) copy-start(bf16[128,512]{1,0:T(8,128)(2,1)} %up_ref.3) | copy-start | bytes 393220
  12.3 5.6 %copy-start.3 = (bf16[512,128]{1,0:T(8,128)(2,1)S(1)}, bf16[512,128]{1,0:T(8,128)(2,1)}, u32[]{:S(2)}) copy-start(bf16[512,128]{1,0:T(8,128)(2,1)} %down_ref.3) | copy-start | bytes 393220
  12.3 5.5 %copy-start.4 = (f32[15,128]{1,0:T(8,128)S(1)}, f32[15,128]{1,0:T(8,128)}, u32[]{:S(2)}) copy-start(f32[15,128]{1,0:T(8,128)} %taps_ref.3) | copy-start | bytes 23044
  12.4 1.6 %collective-permute-start.2 = (bf16[32,32,128]{2,1,0:T(8,128)(2,1)S(1)}, bf16[32,32,128]{2,1,0:T(8,128)(2,1)S(1)}, u32[]{:S(2)}, u32[]{:S(2)}) collective-permute-start(bf16[32,32,128]{2,1,0:T(8,128)(2,1)S(1)} %get-tuple-element.10), channel_id=1, source_target_pairs={{0,1},{1,0},{2,3},{3,2},{4,5},{5,4},{6,7},{7,6},{8,9},{9,8},{10,11... | collective-permute-start | bytes 786440 | tf_op jit(solution)/shard_map/ppermute | solution.py:300
  12.7 5.1 %copy-start.5 = (f32[31]{0:T(128)S(1)}, f32[31]{0:T(128)}, u32[]{:S(2)}) copy-start(f32[31]{0:T(128)} %polar_taps_ref.1) | copy-start | bytes 376
  12.7 5.1 %copy-start.6 = (f32[128]{0:T(128)S(1)}, f32[128]{0:T(128)}, u32[]{:S(2)}) copy-start(f32[128]{0:T(128)} %param.12) | copy-start | bytes 1540
  12.7 1.6 %collective-permute-start.1 = (bf16[32,32,128]{2,1,0:T(8,128)(2,1)S(1)}, bf16[32,32,128]{2,1,0:T(8,128)(2,1)S(1)}, u32[]{:S(2)}, u32[]{:S(2)}) collective-permute-start(bf16[32,32,128]{2,1,0:T(8,128)(2,1)S(1)} %get-tuple-element.11), channel_id=1, source_target_pairs={{0,1},{1,0},{2,3},{3,2},{4,5},{5,4},{6,7},{7,6},{8,9},{9,8},{10,11... | collective-permute-start | bytes 786440 | tf_op jit(solution)/shard_map/ppermute | solution.py:300

commit v4 on v3

--- a/solution.py
+++ b/solution.py
@@ -13,6 +13,7 @@
 PARTS = 1
 SHARES = 2
 VMEM_BYTES = 48 * 1024 * 1024
+PREP_VMEM_BYTES = 62 * 1024 * 1024
 F32 = jnp.float32
 BF16 = jnp.bfloat16
 
@@ -56,24 +57,21 @@
 
 
 def prep_kernel(
-    slots, rows_hbm, owner_hbm, field_hbm, mask_hbm, masked_hbm, out_hbm,
-    rows, owners, count, field, masked, mask_t, mask_f, extra, extra_half, small_sems, load_sems, store_sems, row_sems, extra_sem,
+    slots, rows_hbm, owner_hbm, field_hbm, mask_hbm, masked, out_hbm,
+    rows, owners, count, field, mask_t, mask_f, extra, extra_half, small_sems, load_sem, row_sems, extra_sem,
 ):
     lat_rows, cols, channels = field.shape
     tiles = out_hbm.shape[0]
-    parts = load_sems.shape[0]
-    some = lat_rows // parts
     entries = owners.shape[0]
     small = [
         pltpu.make_async_copy(rows_hbm, rows, small_sems.at[0]),
         pltpu.make_async_copy(owner_hbm, owners, small_sems.at[1]),
         pltpu.make_async_copy(mask_hbm, mask_t, small_sems.at[2]),
     ]
-    blocks = [pl.ds(p * some, some) for p in range(parts)]
-    loads = [pltpu.make_async_copy(field_hbm.at[b], field.at[b], load_sems.at[p]) for p, b in enumerate(blocks)]
-    stores = [pltpu.make_async_copy(masked.at[b], masked_hbm.at[b], store_sems.at[p]) for p, b in enumerate(blocks)]
-    for copy in small + loads:
+    load = pltpu.make_async_copy(field_hbm, field, load_sem)
+    for copy in small:
         copy.start()
+    load.start()
     mask_f[...] = jnp.zeros_like(mask_f)
     extra[...] = jnp.zeros_like(extra)
     for tile in range(tiles):
@@ -101,48 +99,43 @@
     extra_half[...] = extra[...].astype(BF16).reshape(tiles, EXTRA, channels)
     extra_copy = pltpu.make_async_copy(extra_half, out_hbm.at[:, pl.ds(slots * cols, EXTRA)], extra_sem)
     extra_copy.start()
-    for p in range(parts):
-        at = slice(p * some, (p + 1) * some)
-        wide = spread_mask(mask[at], channels).astype(BF16)
-        loads[p].wait()
-        masked[at] = field[at] * wide.reshape(some, cols, channels)
-        stores[p].start()
+    wide = spread_mask(mask, channels).astype(BF16).reshape(lat_rows, cols, channels)
+    load.wait()
+    masked[...] = field[...] * wide
     for e, place in enumerate(places):
         row_copy(e, *place).start()
     for e, place in enumerate(places):
         row_copy(e, *place).wait()
     extra_copy.wait()
-    for store in stores:
-        store.wait()
 
 
 def prep(field, land_mask, polar_rows, polar_owner, tiles, slots):
     lat_rows, cols, channels = field.shape
     hbm = pl.BlockSpec(memory_space=pltpu.HBM)
+    vmem = pl.BlockSpec(memory_space=pltpu.VMEM)
     return pl.pallas_call(
         functools.partial(prep_kernel, slots),
         out_shape=(
-            jax.ShapeDtypeStruct(field.shape, BF16),
+            pltpu.VMEM(field.shape, BF16),
             jax.ShapeDtypeStruct((tiles, slots * cols + EXTRA, channels), BF16),
         ),
         in_specs=[hbm] * 4,
-        out_specs=(hbm, hbm),
+        out_specs=(vmem, hbm),
         scratch_shapes=[
             pltpu.SMEM(polar_rows.shape, jnp.int32),
             pltpu.SMEM(polar_owner.shape, jnp.int32),
             pltpu.SMEM((tiles,), jnp.int32),
-            pltpu.VMEM(field.shape, BF16),
             pltpu.VMEM(field.shape, BF16),
             pltpu.VMEM((cols, lat_rows), jnp.int32),
             pltpu.VMEM((lat_rows, channels), F32),
             pltpu.VMEM((tiles * EXTRA, channels), F32),
             pltpu.VMEM((tiles, EXTRA, channels), BF16),
             pltpu.SemaphoreType.DMA((3,)),
-            pltpu.SemaphoreType.DMA((PARTS,)),
-            pltpu.SemaphoreType.DMA((PARTS,)),
+            pltpu.SemaphoreType.DMA,
             pltpu.SemaphoreType.DMA(polar_owner.shape),
             pltpu.SemaphoreType.DMA,
         ],
+        compiler_params=pltpu.CompilerParams(vmem_limit_bytes=PREP_VMEM_BYTES),
         cost_estimate=pl.CostEstimate(flops=10**6, bytes_accessed=2 * 10**6, transcendentals=0),
         name="prep",
     )(polar_rows, polar_owner, field, land_mask.T)

time: 31.5 us -> 31.2 us (level)
  no operation moved by 1% of the time
where the time goes in v4:
time: 31.2 us; the launch traced here: 31 us
  Pallas kernels  11 us (35%)
  starting transfers between devices  9.66 us (31%)
  waiting for transfers between devices  9.53 us (31%)
  between operations  0.71 us (2%)
    ppermute x1, starting transfers between devices, body(): cross = lax.ppermute(masked, 'lon', cross_pairs)  5.51 us
    all_to_all x1, waiting for transfers between devices, body(): lax.all_to_all(outgoing, 'lon', split_axis=0, concat_axis=0, tiled=True)  4.88 us
    pallas_call x1, Pallas kernels, tile_part(): pl.pallas_call(functools.partial(tile_kernel, 32), out_shape=(jax.ShapeDt...  4.74 us
    pallas_call x1, Pallas kernels, polar_part(): pl.pallas_call(functools.partial(polar_kernel, slots, cols), out_shape=ja...  3.99 us
    all_to_all x1, starting transfers between devices, body(): lax.all_to_all(outgoing, 'lon', split_axis=0, concat_axis=0, tiled=True)  3.58 us
    ppermute x1, waiting for transfers between devices, body(): cross = lax.ppermute(masked, 'lon', cross_pairs)  3.25 us
    pallas_call x1, Pallas kernels, prep(): pl.pallas_call(functools.partial(prep_kernel, slots), out_shape=(pltpu.VM...  2.25 us
    ppermute x1, waiting for transfers between devices, body(): lax.ppermute(masked[half:], 'lon', swap_pairs)  1.02 us
  transfers between devices with their start and end apart: 4, of which 4 were waited for; matrix products, arithmetic and copies ran while one was open for 0% of the time, Pallas kernels for 15%

profile of v4, /device:TPU:0, one launch (start us, length us, event | category | flops | bytes accessed | tf_op | source)
XLA Modules:
  0.0 31.0 jit_solution(1109645029414221550)
XLA Ops:
  0.6 2.3 %prep.1 = (bf16[64,32,128]{2,1,0:T(8,128)(2,1)S(1)}, bf16[16,136,128]{2,1,0:T(8,128)(2,1)}) custom-call(s32[32]{0:T(128)} %rows_hbm.1, s32[32]{0:T(128)} %owner_hbm.1, bf16[64,32,128]{2,1,0:T(8,128)(2,1)} %field_hbm.1, s32[32,64]{1,0:T(8,128)} %bitcast.2), custom_call_target="tpu_custom_call" | custom-call | flops 1000000 | bytes 2000000 | tf_op jit(solution)/shard_map/prep/pallas_call | solution.py:116
  2.9 5.5 %collective-permute-start = (bf16[64,32,128]{2,1,0:T(8,128)(2,1)S(1)}, bf16[64,32,128]{2,1,0:T(8,128)(2,1)S(1)}, u32[]{:S(2)}, u32[]{:S(2)}) collective-permute-start(bf16[64,32,128]{2,1,0:T(8,128)(2,1)S(1)} %get-tuple-element.6.own_ref), channel_id=1, source_target_pairs={{0,15},{1,2},{2,1},{3,4},{4,3},{5,6},{6,5},{7,8},{8,7},{9,10},{10,... | collective-permute-start | bytes 1572872 | tf_op jit(solution)/shard_map/ppermute | solution.py:291
  8.4 3.6 %all-to-all-start = ((bf16[16,136,128]{2,1,0:T(8,128)(2,1)}), bf16[16,136,128]{2,1,0:T(8,128)(2,1)S(1)}, u32[]{:S(2)}, u32[]{:S(2)}) async-start(bf16[16,136,128]{2,1,0:T(8,128)(2,1)} %get-tuple-element.8), calls=%async_computation | async-start | bytes 1114112 | tf_op jit(solution)/shard_map/all_to_all | solution.py:294
  12.0 0.0 copy-start
  12.0 0.0 copy-start.1
  12.0 0.0 copy-start.2
  12.0 0.0 copy-start.3
  12.1 0.4 %collective-permute-start.2 = (bf16[32,32,128]{2,1,0:T(8,128)(2,1)S(1)}, bf16[32,32,128]{2,1,0:T(8,128)(2,1)S(1)}, u32[]{:S(2)}, u32[]{:S(2)}) collective-permute-start(bf16[32,32,128]{2,1,0:T(8,128)(2,1)S(1)} %get-tuple-element.10), channel_id=1, source_target_pairs={{0,1},{1,0},{2,3},{3,2},{4,5},{5,4},{6,7},{7,6},{8,9},{9,8},{10,11... | collective-permute-start | bytes 786440 | tf_op jit(solution)/shard_map/ppermute | solution.py:293
  12.4 0.0 copy-start.4
  12.4 0.0 copy-start.5
  12.4 0.2 collective-permute-start.1
  12.7 1.0 %collective-permute-done.2.lower_ref = bf16[32,32,128]{2,1,0:T(8,128)(2,1)S(1)} collective-permute-done((bf16[32,32,128]{2,1,0:T(8,128)(2,1)S(1)}, bf16[32,32,128]{2,1,0:T(8,128)(2,1)S(1)}, u32[]{:S(2)}, u32[]{:S(2)}) %collective-permute-start.2) | collective-permute-done | bytes 262176 | tf_op jit(solution)/shard_map/ppermute | solution.py:293
  13.7 0.4 %collective-permute-done.1.upper_ref = bf16[32,32,128]{2,1,0:T(8,128)(2,1)S(1)} collective-permute-done((bf16[32,32,128]{2,1,0:T(8,128)(2,1)S(1)}, bf16[32,32,128]{2,1,0:T(8,128)(2,1)S(1)}, u32[]{:S(2)}, u32[]{:S(2)}) %collective-permute-start.1) | collective-permute-done | bytes 262176 | tf_op jit(solution)/shard_map/ppermute | solution.py:293
  14.1 3.3 %collective-permute-done.cross_ref = bf16[64,32,128]{2,1,0:T(8,128)(2,1)S(1)} collective-permute-done((bf16[64,32,128]{2,1,0:T(8,128)(2,1)S(1)}, bf16[64,32,128]{2,1,0:T(8,128)(2,1)S(1)}, u32[]{:S(2)}, u32[]{:S(2)}) %collective-permute-start) | collective-permute-done | bytes 524320 | tf_op jit(solution)/shard_map/ppermute | solution.py:291
  17.3 0.0 copy-done
  17.3 0.0 copy-done.1
  17.3 0.0 copy-done.2
  17.3 0.0 copy-done.3
  17.3 0.0 copy-done.4
  17.3 0.0 copy-done.5
  17.3 4.7 %tile.1 = (bf16[64,32,128]{2,1,0:T(8,128)(2,1)}, bf16[256,160]{1,0:T(8,128)(2,1)S(1)}) custom-call(f32[31]{0:T(128)S(1)} %copy-done.4, bf16[64,32,128]{2,1,0:T(8,128)(2,1)S(1)} %get-tuple-element.6.own_ref, bf16[64,32,128]{2,1,0:T(8,128)(2,1)S(1)} %collective-permute-done.cross_ref, bf16[32,32,128]{2,1,0:T(8,128)(2,1)S(1)} %collective-permute-done.1.upper_ref, ...), custom_call_target="tpu_custom_call" | custom-call | flops 7000000000 | bytes 3000000 | tf_op jit(solution)/shard_map/tile/pallas_call | solution.py:195
  22.1 4.9 %all-to-all-done.recv_ref = bf16[16,136,128]{2,1,0:T(8,128)(2,1)S(1)} async-done(((bf16[16,136,128]{2,1,0:T(8,128)(2,1)}), bf16[16,136,128]{2,1,0:T(8,128)(2,1)S(1)}, u32[]{:S(2)}, u32[]{:S(2)}) %all-to-all-start) | async-done | bytes 557088 | tf_op jit(solution)/shard_map/all_to_all | solution.py:294
  27.0 4.0 %polar.1 = bf16[4,512,128]{2,1,0:T(8,128)(2,1)} custom-call(bf16[16,136,128]{2,1,0:T(8,128)(2,1)S(1)} %all-to-all-done.recv_ref, bf16[256,160]{1,0:T(8,128)(2,1)S(1)} %get-tuple-element.9.bands_ref, f32[15,128]{1,0:T(8,128)S(1)} %copy-done.3, f32[1,128]{1,0:T(1,128)S(1)} %bitcast.5, bf16[128,512]{1,0:T(8,128)(2,1)S(1)} %copy-done.1, ...), custom_call_target="tpu_custom_call" | custom-call | flops 600000000 | bytes 2000000 | tf_op jit(solution)/shard_map/polar/pallas_call | solution.py:252
  (1 shorter events, 0.0 us)
Async XLA Ops:
  2.9 14.4 %collective-permute-start = (bf16[64,32,128]{2,1,0:T(8,128)(2,1)S(1)}, bf16[64,32,128]{2,1,0:T(8,128)(2,1)S(1)}, u32[]{:S(2)}, u32[]{:S(2)}) collective-permute-start(bf16[64,32,128]{2,1,0:T(8,128)(2,1)S(1)} %get-tuple-element.6.own_ref), channel_id=1, source_target_pairs={{0,15},{1,2},{2,1},{3,4},{4,3},{5,6},{6,5},{7,8},{8,7},{9,10},{10,... | collective-permute-start | bytes 1572872 | tf_op jit(solution)/shard_map/ppermute | solution.py:291
  8.4 18.6 %all-to-all-start = ((bf16[16,136,128]{2,1,0:T(8,128)(2,1)}), bf16[16,136,128]{2,1,0:T(8,128)(2,1)S(1)}, u32[]{:S(2)}, u32[]{:S(2)}) async-start(bf16[16,136,128]{2,1,0:T(8,128)(2,1)} %get-tuple-element.8), calls=%async_computation | async-start | bytes 1114112 | tf_op jit(solution)/shard_map/all_to_all | solution.py:294
  12.0 5.3 %copy-start = (s32[64,32]{0,1:T(8,128)S(1)}, s32[64,32]{0,1:T(8,128)}, u32[]{:S(2)}) copy-start(s32[64,32]{0,1:T(8,128)} %param.10) | copy-start | bytes 24580
  12.0 5.3 %copy-start.1 = (bf16[128,512]{1,0:T(8,128)(2,1)S(1)}, bf16[128,512]{1,0:T(8,128)(2,1)}, u32[]{:S(2)}) copy-start(bf16[128,512]{1,0:T(8,128)(2,1)} %up_ref.3) | copy-start | bytes 393220
  12.0 5.3 %copy-start.2 = (bf16[512,128]{1,0:T(8,128)(2,1)S(1)}, bf16[512,128]{1,0:T(8,128)(2,1)}, u32[]{:S(2)}) copy-start(bf16[512,128]{1,0:T(8,128)(2,1)} %down_ref.3) | copy-start | bytes 393220
  12.0 5.3 %copy-start.3 = (f32[15,128]{1,0:T(8,128)S(1)}, f32[15,128]{1,0:T(8,128)}, u32[]{:S(2)}) copy-start(f32[15,128]{1,0:T(8,128)} %taps_ref.3) | copy-start | bytes 23044
  12.1 1.6 %collective-permute-start.2 = (bf16[32,32,128]{2,1,0:T(8,128)(2,1)S(1)}, bf16[32,32,128]{2,1,0:T(8,128)(2,1)S(1)}, u32[]{:S(2)}, u32[]{:S(2)}) collective-permute-start(bf16[32,32,128]{2,1,0:T(8,128)(2,1)S(1)} %get-tuple-element.10), channel_id=1, source_target_pairs={{0,1},{1,0},{2,3},{3,2},{4,5},{5,4},{6,7},{7,6},{8,9},{9,8},{10,11... | collective-permute-start | bytes 786440 | tf_op jit(solution)/shard_map/ppermute | solution.py:293
  12.4 4.9 %copy-start.4 = (f32[31]{0:T(128)S(1)}, f32[31]{0:T(128)}, u32[]{:S(2)}) copy-start(f32[31]{0:T(128)} %polar_taps_ref.1) | copy-start | bytes 376
  12.4 4.9 %copy-start.5 = (f32[128]{0:T(128)S(1)}, f32[128]{0:T(128)}, u32[]{:S(2)}) copy-start(f32[128]{0:T(128)} %param.12) | copy-start | bytes 1540
  12.4 1.6 %collective-permute-start.1 = (bf16[32,32,128]{2,1,0:T(8,128)(2,1)S(1)}, bf16[32,32,128]{2,1,0:T(8,128)(2,1)S(1)}, u32[]{:S(2)}, u32[]{:S(2)}) collective-permute-start(bf16[32,32,128]{2,1,0:T(8,128)(2,1)S(1)} %get-tuple-element.11), channel_id=1, source_target_pairs={{0,1},{1,0},{2,3},{3,2},{4,5},{5,4},{6,7},{7,6},{8,9},{9,8},{10,11... | collective-permute-start | bytes 786440 | tf_op jit(solution)/shard_map/ppermute | solution.py:293

commit v5 on v4

--- a/solution.py
+++ b/solution.py
@@ -28,9 +28,11 @@
     return jnp.dot(picked, jnp.ones((cols, channels), BF16), preferred_element_type=F32)
 
 
-def branch_rows(triples, taps, gain, up, down):
+def branch_rows(triples, table, up, down):
     zonal = []
-    n_taps = len(taps)
+    n_taps = table.shape[0] - 1
+    taps = [table[k : k + 1] for k in range(n_taps)]
+    gain = table[n_taps:]
     for left, own, right in triples:
         cols = own.shape[0]
         start = cols - n_taps // 2 * DILATION_STEP
@@ -141,41 +143,13 @@
     )(polar_rows, polar_owner, field, land_mask.T)
 
 
-def tile_kernel(
-    chunk, polar_taps_ref, own_ref, cross_ref, upper_ref, lower_ref, mask_ref, taps_ref, gain_ref, up_ref, down_ref,
-    mixed_ref, bands_ref, left, right, mask_f,
-):
-    lat_rows, cols, channels = own_ref.shape
-    half = lat_rows // 2
-    odd = lax.rem(lax.axis_index("lon"), 2)
-
-    @pl.when(odd == 0)
-    def _():
-        left[...] = cross_ref[...]
-        right[:half] = upper_ref[...]
-        right[half:] = lower_ref[...]
-
-    @pl.when(odd == 1)
-    def _():
-        left[:half] = upper_ref[...]
-        left[half:] = lower_ref[...]
-        right[...] = cross_ref[...]
-
+def side_kernel(polar_taps_ref, mask_ref, upper_ref, lower_ref, taps_ref, gain_ref, mask_f, near, table, bands_ref):
+    half = upper_ref.shape[0]
     mask_f[...] = mask_ref[...].astype(F32).T
-
-    def some_rows(step, _):
-        at = pl.ds(step * chunk, chunk)
-        triples = [(left[step * chunk + r], own_ref[step * chunk + r], right[step * chunk + r]) for r in range(chunk)]
-        taps = [taps_ref[k : k + 1] for k in range(taps_ref.shape[0])]
-        branch = branch_rows(triples, taps, gain_ref[...], up_ref[...], down_ref[...])
-        wide = spread_mask(mask_f[at, :], channels)
-        own = own_ref[at].reshape(chunk * cols, channels).astype(F32)
-        mixed = wide * (own + branch.astype(BF16).astype(F32))
-        mixed_ref[at] = mixed.astype(BF16).reshape(chunk, cols, channels)
-        return 0
-
-    lax.fori_loop(0, lat_rows // chunk, some_rows, 0)
-
+    near[:half] = upper_ref[...]
+    near[half:] = lower_ref[...]
+    table[: taps_ref.shape[0]] = taps_ref[...]
+    table[taps_ref.shape[0] :] = gain_ref[...]
     n, depth = bands_ref.shape[0] // 2, bands_ref.shape[1]
     n_taps = polar_taps_ref.shape[0]
     offset = lax.broadcasted_iota(jnp.int32, (n, depth), 1) - lax.broadcasted_iota(jnp.int32, (n, depth), 0)
@@ -188,43 +162,77 @@
     bands_ref[n:] = (band - high.astype(F32)).astype(BF16)
 
 
-def tile_part(polar_taps, masked, cross, swaps, land_mask, weights):
-    lat_rows, cols, channels = masked.shape
+def side_part(polar_taps, land_mask, swaps, zonal_tap_weight, norm_gain):
+    lat_rows, cols = land_mask.shape
     smem = pl.BlockSpec(memory_space=pltpu.SMEM)
     vmem = pl.BlockSpec(memory_space=pltpu.VMEM)
+    half, _, channels = swaps[0].shape
     return pl.pallas_call(
-        functools.partial(tile_kernel, 32),
+        side_kernel,
         out_shape=(
-            jax.ShapeDtypeStruct(masked.shape, BF16),
+            jax.ShapeDtypeStruct((lat_rows, cols), F32),
+            jax.ShapeDtypeStruct((2 * half, cols, channels), BF16),
+            jax.ShapeDtypeStruct((zonal_tap_weight.shape[0] + 1, channels), F32),
             jax.ShapeDtypeStruct((256, 160), BF16),
         ),
-        in_specs=[smem] + [vmem] * 9,
-        out_specs=(vmem, vmem),
-        scratch_shapes=[pltpu.VMEM(masked.shape, BF16)] * 2 + [pltpu.VMEM((lat_rows, cols), F32)],
+        in_specs=[smem] + [vmem] * 5,
+        out_specs=(vmem,) * 4,
+        compiler_params=pltpu.CompilerParams(vmem_limit_bytes=VMEM_BYTES),
+        cost_estimate=pl.CostEstimate(flops=10**6, bytes_accessed=10**6, transcendentals=0),
+        name="side",
+    )(polar_taps, land_mask.T, *swaps, zonal_tap_weight, norm_gain.reshape(1, channels))
+
+
+def tile_kernel(own_ref, cross_ref, near_ref, mask_ref, table_ref, up_ref, down_ref, mixed_ref):
+    lat_rows, cols, channels = own_ref.shape
+    odd = lax.rem(lax.axis_index("lon"), 2)
+
+    def all_rows(left, right):
+        triples = [(left[r], own_ref[r], right[r]) for r in range(lat_rows)]
+        branch = branch_rows(triples, table_ref[...], up_ref[...], down_ref[...])
+        wide = spread_mask(mask_ref[...], channels)
+        own = own_ref[...].reshape(lat_rows * cols, channels).astype(F32)
+        mixed = wide * (own + branch.astype(BF16).astype(F32))
+        mixed_ref[...] = mixed.astype(BF16).reshape(lat_rows, cols, channels)
+
+    pl.when(odd == 0)(functools.partial(all_rows, cross_ref, near_ref))
+    pl.when(odd == 1)(functools.partial(all_rows, near_ref, cross_ref))
+
+
+def tile_part(masked, cross, near, mask_f, weights):
+    vmem = pl.BlockSpec(memory_space=pltpu.VMEM)
+    return pl.pallas_call(
+        tile_kernel,
+        out_shape=jax.ShapeDtypeStruct(masked.shape, BF16),
+        in_specs=[vmem] * 7,
+        out_specs=vmem,
         compiler_params=pltpu.CompilerParams(vmem_limit_bytes=VMEM_BYTES),
         cost_estimate=pl.CostEstimate(flops=TILE_FLOPS, bytes_accessed=3 * 10**6, transcendentals=10**6),
         name="tile",
-    )(polar_taps, masked, cross, *swaps, land_mask.T, *weights)
+    )(masked, cross, near, mask_f, *weights)
 
 
 def polar_kernel(
-    slots, cols, recv_ref, bands_ref, taps_ref, gain_ref, up_ref, down_ref,
+    slots, cols, recv_ref, bands_ref, table_ref, up_ref, down_ref,
     out_hbm, circle, out, sems,
 ):
     tiles, _, channels = recv_ref.shape
     n, depth = bands_ref.shape[0] // 2, bands_ref.shape[1]
     pad = (depth - n) // 2
     nlon = tiles * cols
-    taps = [taps_ref[k : k + 1] for k in range(taps_ref.shape[0])]
     extra = recv_ref[:, slots * cols :, :].astype(F32)
-    copies = []
     share = nlon // n // SHARES
-    for pair in range(slots // 2):
+
+    def out_copy(pair, part):
+        at = (pl.ds(pair * 2, 2), pl.ds(part * share * n, share * n))
+        return pltpu.make_async_copy(out.at[at], out_hbm.at[at], sems.at[pair, part])
+
+    def filter_pair(pair):
         for half in range(2):
             slot = pair * 2 + half
             pieces = [recv_ref[t, slot * cols : (slot + 1) * cols, :].astype(F32) for t in range(tiles)]
             triples = [(pieces[t - 1], pieces[t], pieces[(t + 1) % tiles]) for t in range(tiles)]
-            branch = branch_rows(triples, taps, gain_ref[...], up_ref[...], down_ref[...])
+            branch = branch_rows(triples, table_ref[...], up_ref[...], down_ref[...])
             wide = spread_mask(extra[:, slot, :cols], channels)
             own = jnp.concatenate(pieces, axis=0)
             mixed = jnp.where(wide > 0.5, own + branch.astype(BF16).astype(F32), 0.0).astype(BF16)
@@ -238,11 +246,33 @@
             for half in range(2):
                 out[pair * 2 + half, b * n : (b + 1) * n, :] = rows[:, half * channels : (half + 1) * channels]
             if (b + 1) % share == 0:
-                at = (pl.ds(pair * 2, 2), pl.ds((b + 1 - share) * n, share * n))
-                copies.append(pltpu.make_async_copy(out.at[at], out_hbm.at[at], sems.at[len(copies)]))
-                copies[-1].start()
-    for copy in copies:
-        copy.wait()
+                out_copy(pair, b // share).start()
+
+    def clear_pair(pair):
+        out[pair * 2 : pair * 2 + 2] = jnp.zeros_like(out[pair * 2 : pair * 2 + 2])
+        for part in range(SHARES):
+            out_copy(pair, part).start()
+
+    pairs = slots // 2
+
+    def all_pairs():
+        for pair in range(pairs):
+            filter_pair(pair)
+
+    def first_pair():
+        for pair in range(1, pairs):
+            clear_pair(pair)
+        filter_pair(0)
+
+    if pairs > 1:
+        ocean = jnp.max(extra[:, 2:slots, :])
+        pl.when(ocean > 0.5)(all_pairs)
+        pl.when(jnp.logical_not(ocean > 0.5))(first_pair)
+    else:
+        all_pairs()
+    for pair in range(pairs):
+        for part in range(SHARES):
+            out_copy(pair, part).wait()
 
 
 def polar_part(recv, bands, weights, slots, cols):
@@ -252,12 +282,12 @@
     return pl.pallas_call(
         functools.partial(polar_kernel, slots, cols),
         out_shape=jax.ShapeDtypeStruct(shape, BF16),
-        in_specs=[vmem] * 6,
+        in_specs=[vmem] * 5,
         out_specs=pl.BlockSpec(memory_space=pltpu.HBM),
         scratch_shapes=[
             pltpu.VMEM((slots // 2, tiles * cols + 32, 2 * channels), BF16),
             pltpu.VMEM(shape, BF16),
-            pltpu.SemaphoreType.DMA((slots // 2 * SHARES,)),
+            pltpu.SemaphoreType.DMA((slots // 2, SHARES)),
         ],
         compiler_params=pltpu.CompilerParams(vmem_limit_bytes=VMEM_BYTES),
         cost_estimate=pl.CostEstimate(flops=6 * 10**8, bytes_accessed=2 * 10**6, transcendentals=10**6),
@@ -279,12 +309,6 @@
     lat_rows, cols, channels = field.shape
     tiles = lax.axis_size("lon")
     slots = max(2, lat_rows // tiles)
-    weights = (
-        zonal_tap_weight,
-        norm_gain.reshape(1, channels),
-        up_weight,
-        down_weight,
-    )
     masked, outgoing = prep(field, land_mask, polar_rows, polar_owner, tiles, slots)
     swap_pairs = [(i, i ^ 1) for i in range(tiles)]
     cross_pairs = [(i, (i + 1) % tiles if i % 2 else (i - 1) % tiles) for i in range(tiles)]
@@ -292,7 +316,9 @@
     half = lat_rows // 2
     swaps = [lax.ppermute(masked[:half], "lon", swap_pairs), lax.ppermute(masked[half:], "lon", swap_pairs)]
     recv = lax.all_to_all(outgoing, "lon", split_axis=0, concat_axis=0, tiled=True)
-    mixed, bands = tile_part(polar_taps, masked, cross, swaps, land_mask, weights)
+    mask_f, near, table, bands = side_part(polar_taps, land_mask, swaps, zonal_tap_weight, norm_gain)
+    weights = (table, up_weight, down_weight)
+    mixed = tile_part(masked, cross, near, mask_f, weights)
     polar = polar_part(recv, bands, weights, slots, cols)
     return (mixed, polar)
 

time: 31.2 us -> 30.6 us (0.981)
  the two profiles are of different devices: /device:TPU:0 before, /device:TPU:29 now
where the time goes in v5:
time: 30.6 us; the launch traced here: 30.4 us
  Pallas kernels  11 us (36%)
  waiting for transfers between devices  10.1 us (33%)
  starting transfers between devices  8.56 us (28%)
  between operations  0.71 us (2%)
    all_to_all x1, starting transfers between devices, body(): lax.all_to_all(outgoing, 'lon', split_axis=0, concat_axis=0, tiled=True)  7.92 us
    all_to_all x1, waiting for transfers between devices, body(): lax.all_to_all(outgoing, 'lon', split_axis=0, concat_axis=0, tiled=True)  5.7 us
    pallas_call x1, Pallas kernels, polar_part(): pl.pallas_call(functools.partial(polar_kernel, slots, cols), out_shape=ja...  4.11 us
    pallas_call x1, Pallas kernels, tile_part(): pl.pallas_call(tile_kernel, out_shape=jax.ShapeDtypeStruct(masked.shape,...  3.91 us
    ppermute x1, waiting for transfers between devices, body(): cross = lax.ppermute(masked, 'lon', cross_pairs)  2.98 us
    pallas_call x1, Pallas kernels, prep(): pl.pallas_call(functools.partial(prep_kernel, slots), out_shape=(pltpu.VM...  2.25 us
    ppermute x1, waiting for transfers between devices, body(): lax.ppermute(masked[half:], 'lon', swap_pairs)  1.02 us
    pallas_call x1, Pallas kernels, side_part(): pl.pallas_call(side_kernel, out_shape=(jax.ShapeDtypeStruct((lat_rows, co...  0.71 us
  transfers between devices with their start and end apart: 4, of which 4 were waited for; matrix products, arithmetic and copies ran while one was open for 0% of the time, Pallas kernels for 15%

profile of v5, /device:TPU:29, one launch (start us, length us, event | category | flops | bytes accessed | tf_op | source)
XLA Modules:
  0.0 30.4 jit_solution(17705460413692038129)
XLA Ops:
  0.6 2.3 %prep.1 = (bf16[64,32,128]{2,1,0:T(8,128)(2,1)S(1)}, bf16[16,136,128]{2,1,0:T(8,128)(2,1)}) custom-call(s32[32]{0:T(128)} %rows_hbm.1, s32[32]{0:T(128)} %owner_hbm.1, bf16[64,32,128]{2,1,0:T(8,128)(2,1)} %field_hbm.1, s32[32,64]{1,0:T(8,128)} %bitcast.2), custom_call_target="tpu_custom_call" | custom-call | flops 1000000 | bytes 2000000 | tf_op jit(solution)/shard_map/prep/pallas_call | solution.py:118
  2.9 0.1 collective-permute-start
  3.0 7.9 %all-to-all-start = ((bf16[16,136,128]{2,1,0:T(8,128)(2,1)}), bf16[16,136,128]{2,1,0:T(8,128)(2,1)S(1)}, u32[]{:S(2)}, u32[]{:S(2)}) async-start(bf16[16,136,128]{2,1,0:T(8,128)(2,1)} %get-tuple-element.12), calls=%async_computation | async-start | bytes 1114112 | tf_op jit(solution)/shard_map/all_to_all | solution.py:318
  10.9 0.0 copy-start
  10.9 0.0 copy-start.1
  10.9 0.4 %collective-permute-start.2 = (bf16[32,32,128]{2,1,0:T(8,128)(2,1)S(1)}, bf16[32,32,128]{2,1,0:T(8,128)(2,1)S(1)}, u32[]{:S(2)}, u32[]{:S(2)}) collective-permute-start(bf16[32,32,128]{2,1,0:T(8,128)(2,1)S(1)} %get-tuple-element.14), channel_id=1, source_target_pairs={{0,1},{1,0},{2,3},{3,2},{4,5},{5,4},{6,7},{7,6},{8,9},{9,8},{10,11... | collective-permute-start | bytes 786440 | tf_op jit(solution)/shard_map/ppermute | solution.py:317
  11.4 0.0 copy-start.2
  11.4 0.0 copy-start.3
  11.4 0.1 collective-permute-start.1
  11.5 1.0 %collective-permute-done.2.lower_ref = bf16[32,32,128]{2,1,0:T(8,128)(2,1)S(1)} collective-permute-done((bf16[32,32,128]{2,1,0:T(8,128)(2,1)S(1)}, bf16[32,32,128]{2,1,0:T(8,128)(2,1)S(1)}, u32[]{:S(2)}, u32[]{:S(2)}) %collective-permute-start.2) | collective-permute-done | bytes 262176 | tf_op jit(solution)/shard_map/ppermute | solution.py:317
  12.6 0.4 %collective-permute-done.1.upper_ref = bf16[32,32,128]{2,1,0:T(8,128)(2,1)S(1)} collective-permute-done((bf16[32,32,128]{2,1,0:T(8,128)(2,1)S(1)}, bf16[32,32,128]{2,1,0:T(8,128)(2,1)S(1)}, u32[]{:S(2)}, u32[]{:S(2)}) %collective-permute-start.1) | collective-permute-done | bytes 262176 | tf_op jit(solution)/shard_map/ppermute | solution.py:317
  12.9 0.0 copy-done
  12.9 0.0 copy-done.1
  12.9 0.0 copy-done.2
  12.9 0.0 copy-done.3
  12.9 0.0 copy-start.4
  13.0 0.0 copy-start.5
  13.0 0.7 %side.1 = (f32[64,32]{1,0:T(8,128)S(1)}, bf16[64,32,128]{2,1,0:T(8,128)(2,1)S(1)}, f32[16,128]{1,0:T(8,128)S(1)}, bf16[256,160]{1,0:T(8,128)(2,1)S(1)}) custom-call(f32[31]{0:T(128)S(1)} %copy-done.2, s32[32,64]{1,0:T(8,128)S(1)} %bitcast.3, bf16[32,32,128]{2,1,0:T(8,128)(2,1)S(1)} %collective-permute-done.1.upper_ref, ...), custom_call_target="tpu_custom_call" | custom-call | flops 1000000 | bytes 1000000 | tf_op jit(solution)/shard_map/side/pallas_call | solution.py:170
  13.7 3.0 %collective-permute-done.cross_ref = bf16[64,32,128]{2,1,0:T(8,128)(2,1)S(1)} collective-permute-done((bf16[64,32,128]{2,1,0:T(8,128)(2,1)S(1)}, bf16[64,32,128]{2,1,0:T(8,128)(2,1)S(1)}, u32[]{:S(2)}, u32[]{:S(2)}) %collective-permute-start) | collective-permute-done | bytes 524320 | tf_op jit(solution)/shard_map/ppermute | solution.py:315
  16.7 0.0 copy-done.4
  16.7 0.0 copy-done.5
  16.7 3.9 %tile.1 = bf16[64,32,128]{2,1,0:T(8,128)(2,1)} custom-call(bf16[64,32,128]{2,1,0:T(8,128)(2,1)S(1)} %get-tuple-element.8.own_ref, bf16[64,32,128]{2,1,0:T(8,128)(2,1)S(1)} %collective-permute-done.cross_ref, bf16[64,32,128]{2,1,0:T(8,128)(2,1)S(1)} %get-tuple-element.9.near_ref, f32[64,32]{1,0:T(8,128)S(1)} %get-tuple-element.10.mask_ref, ...), custom_call_target="tpu_custom_call" | custom-call | flops 7000000000 | bytes 3000000 | tf_op jit(solution)/shard_map/tile/pallas_call | solution.py:204
  20.6 5.7 %all-to-all-done.recv_ref = bf16[16,136,128]{2,1,0:T(8,128)(2,1)S(1)} async-done(((bf16[16,136,128]{2,1,0:T(8,128)(2,1)}), bf16[16,136,128]{2,1,0:T(8,128)(2,1)S(1)}, u32[]{:S(2)}, u32[]{:S(2)}) %all-to-all-start) | async-done | bytes 557088 | tf_op jit(solution)/shard_map/all_to_all | solution.py:318
  26.3 4.1 %polar.1 = bf16[4,512,128]{2,1,0:T(8,128)(2,1)} custom-call(bf16[16,136,128]{2,1,0:T(8,128)(2,1)S(1)} %all-to-all-done.recv_ref, bf16[256,160]{1,0:T(8,128)(2,1)S(1)} %get-tuple-element.13.bands_ref, f32[16,128]{1,0:T(8,128)S(1)} %get-tuple-element.11.table_ref, bf16[128,512]{1,0:T(8,128)(2,1)S(1)} %copy-done.4, bf16[512,128]{1,0:T(8,128)(2,1)S(1)} %copy-done.5), custom_call_target="tpu_custom_call" | custom-call | flops 600000000 | bytes 2000000 | tf_op jit(solution)/shard_map/polar/pallas_call | solution.py:282
  (1 shorter events, 0.0 us)
Async XLA Ops:
  2.9 13.8 %collective-permute-start = (bf16[64,32,128]{2,1,0:T(8,128)(2,1)S(1)}, bf16[64,32,128]{2,1,0:T(8,128)(2,1)S(1)}, u32[]{:S(2)}, u32[]{:S(2)}) collective-permute-start(bf16[64,32,128]{2,1,0:T(8,128)(2,1)S(1)} %get-tuple-element.8.own_ref), channel_id=1, source_target_pairs={{0,15},{1,2},{2,1},{3,4},{4,3},{5,6},{6,5},{7,8},{8,7},{9,10},{10,... | collective-permute-start | bytes 1572872 | tf_op jit(solution)/shard_map/ppermute | solution.py:315
  3.0 23.3 %all-to-all-start = ((bf16[16,136,128]{2,1,0:T(8,128)(2,1)}), bf16[16,136,128]{2,1,0:T(8,128)(2,1)S(1)}, u32[]{:S(2)}, u32[]{:S(2)}) async-start(bf16[16,136,128]{2,1,0:T(8,128)(2,1)} %get-tuple-element.12), calls=%async_computation | async-start | bytes 1114112 | tf_op jit(solution)/shard_map/all_to_all | solution.py:318
  10.9 2.0 %copy-start = (s32[64,32]{0,1:T(8,128)S(1)}, s32[64,32]{0,1:T(8,128)}, u32[]{:S(2)}) copy-start(s32[64,32]{0,1:T(8,128)} %param.10) | copy-start | bytes 24580
  10.9 2.0 %copy-start.1 = (f32[15,128]{1,0:T(8,128)S(1)}, f32[15,128]{1,0:T(8,128)}, u32[]{:S(2)}) copy-start(f32[15,128]{1,0:T(8,128)} %taps_ref.1) | copy-start | bytes 23044
  10.9 1.6 %collective-permute-start.2 = (bf16[32,32,128]{2,1,0:T(8,128)(2,1)S(1)}, bf16[32,32,128]{2,1,0:T(8,128)(2,1)S(1)}, u32[]{:S(2)}, u32[]{:S(2)}) collective-permute-start(bf16[32,32,128]{2,1,0:T(8,128)(2,1)S(1)} %get-tuple-element.14), channel_id=1, source_target_pairs={{0,1},{1,0},{2,3},{3,2},{4,5},{5,4},{6,7},{7,6},{8,9},{9,8},{10,11... | collective-permute-start | bytes 786440 | tf_op jit(solution)/shard_map/ppermute | solution.py:317
  11.4 1.6 %copy-start.2 = (f32[31]{0:T(128)S(1)}, f32[31]{0:T(128)}, u32[]{:S(2)}) copy-start(f32[31]{0:T(128)} %polar_taps_ref.1) | copy-start | bytes 376
  11.4 1.6 %copy-start.3 = (f32[128]{0:T(128)S(1)}, f32[128]{0:T(128)}, u32[]{:S(2)}) copy-start(f32[128]{0:T(128)} %param.12) | copy-start | bytes 1540
  11.4 1.5 %collective-permute-start.1 = (bf16[32,32,128]{2,1,0:T(8,128)(2,1)S(1)}, bf16[32,32,128]{2,1,0:T(8,128)(2,1)S(1)}, u32[]{:S(2)}, u32[]{:S(2)}) collective-permute-start(bf16[32,32,128]{2,1,0:T(8,128)(2,1)S(1)} %get-tuple-element.15), channel_id=1, source_target_pairs={{0,1},{1,0},{2,3},{3,2},{4,5},{5,4},{6,7},{7,6},{8,9},{9,8},{10,11... | collective-permute-start | bytes 786440 | tf_op jit(solution)/shard_map/ppermute | solution.py:317
  12.9 3.7 %copy-start.4 = (bf16[128,512]{1,0:T(8,128)(2,1)S(1)}, bf16[128,512]{1,0:T(8,128)(2,1)}, u32[]{:S(2)}) copy-start(bf16[128,512]{1,0:T(8,128)(2,1)} %up_ref.3) | copy-start | bytes 393220
  13.0 3.7 %copy-start.5 = (bf16[512,128]{1,0:T(8,128)(2,1)S(1)}, bf16[512,128]{1,0:T(8,128)(2,1)}, u32[]{:S(2)}) copy-start(bf16[512,128]{1,0:T(8,128)(2,1)} %down_ref.3) | copy-start | bytes 393220

commit v6 on v5

--- a/solution.py
+++ b/solution.py
@@ -58,6 +58,10 @@
     return jnp.dot(twice, down, preferred_element_type=F32) * 0.5
 
 
+def lead(tiles):
+    return tiles * 7 // 16
+
+
 def prep_kernel(
     slots, rows_hbm, owner_hbm, field_hbm, mask_hbm, masked, out_hbm,
     rows, owners, count, field, mask_t, mask_f, extra, extra_half, small_sems, load_sem, row_sems, extra_sem,
@@ -92,7 +96,7 @@
     mask_f[:, :cols] = mask
     places = []
     for e in range(entries):
-        owner = owners[e]
+        owner = lax.rem(owners[e] + tiles - lead(tiles), tiles)
         row = rows[e]
         rank = count[owner]
         count[owner] = rank + 1
@@ -220,7 +224,9 @@
     n, depth = bands_ref.shape[0] // 2, bands_ref.shape[1]
     pad = (depth - n) // 2
     nlon = tiles * cols
+    first = lead(tiles)
     extra = recv_ref[:, slots * cols :, :].astype(F32)
+    extra = jnp.concatenate([extra[tiles - first :], extra[: tiles - first]], axis=0)
     share = nlon // n // SHARES
 
     def out_copy(pair, part):
@@ -230,7 +236,9 @@
     def filter_pair(pair):
         for half in range(2):
             slot = pair * 2 + half
-            pieces = [recv_ref[t, slot * cols : (slot + 1) * cols, :].astype(F32) for t in range(tiles)]
+            pieces = [
+                recv_ref[(t - first) % tiles, slot * cols : (slot + 1) * cols, :].astype(F32) for t in range(tiles)
+            ]
             triples = [(pieces[t - 1], pieces[t], pieces[(t + 1) % tiles]) for t in range(tiles)]
             branch = branch_rows(triples, table_ref[...], up_ref[...], down_ref[...])
             wide = spread_mask(extra[:, slot, :cols], channels)
@@ -315,7 +323,10 @@
     cross = lax.ppermute(masked, "lon", cross_pairs)
     half = lat_rows // 2
     swaps = [lax.ppermute(masked[:half], "lon", swap_pairs), lax.ppermute(masked[half:], "lon", swap_pairs)]
-    recv = lax.all_to_all(outgoing, "lon", split_axis=0, concat_axis=0, tiled=True)
+    order = [(lead(tiles) + i) % tiles for i in range(tiles)]
+    recv = lax.all_to_all(
+        outgoing, "lon", split_axis=0, concat_axis=0, axis_index_groups=[order], tiled=True
+    )
     mask_f, near, table, bands = side_part(polar_taps, land_mask, swaps, zonal_tap_weight, norm_gain)
     weights = (table, up_weight, down_weight)
     mixed = tile_part(masked, cross, near, mask_f, weights)

time: 30.6 us -> 30.8 us (level)
  waiting for transfers between devices: 10.1 us -> 12.1 us
  starting transfers between devices: 8.56 us -> 6.68 us
    all_to_all x1, starting transfers between devices: 7.92 us -> 6.04 us  [body(): lax.all_to_all(outgoing, 'lon', split_axis=0, concat_axis=0, axis_index_g...]
    ppermute x1, waiting for transfers between devices: 2.98 us -> 4.42 us  [body(): cross = lax.ppermute(masked, 'lon', cross_pairs)]
    all_to_all x1, waiting for transfers between devices: 5.7 us -> 6.29 us  [body(): lax.all_to_all(outgoing, 'lon', split_axis=0, concat_axis=0, axis_index_g...]
where the time goes in v6:
time: 30.8 us; the launch traced here: 30.5 us
  waiting for transfers between devices  12.1 us (39%)
  Pallas kernels  11 us (36%)
  starting transfers between devices  6.68 us (22%)
  between operations  0.71 us (2%)
    all_to_all x1, waiting for transfers between devices, body(): lax.all_to_all(outgoing, 'lon', split_axis=0, concat_axis=0, axis_index_g...  6.29 us
    all_to_all x1, starting transfers between devices, body(): lax.all_to_all(outgoing, 'lon', split_axis=0, concat_axis=0, axis_index_g...  6.04 us
    ppermute x1, waiting for transfers between devices, body(): cross = lax.ppermute(masked, 'lon', cross_pairs)  4.42 us
    pallas_call x1, Pallas kernels, polar_part(): pl.pallas_call(functools.partial(polar_kernel, slots, cols), out_shape=ja...  4.11 us
    pallas_call x1, Pallas kernels, tile_part(): pl.pallas_call(tile_kernel, out_shape=jax.ShapeDtypeStruct(masked.shape,...  3.91 us
    pallas_call x1, Pallas kernels, prep(): pl.pallas_call(functools.partial(prep_kernel, slots), out_shape=(pltpu.VM...  2.24 us
    ppermute x1, waiting for transfers between devices, body(): lax.ppermute(masked[half:], 'lon', swap_pairs)  1.02 us
    pallas_call x1, Pallas kernels, side_part(): pl.pallas_call(side_kernel, out_shape=(jax.ShapeDtypeStruct((lat_rows, co...  0.71 us
  transfers between devices with their start and end apart: 4, of which 4 were waited for; matrix products, arithmetic and copies ran while one was open for 0% of the time, Pallas kernels for 15%

profile of v6, /device:TPU:29, one launch (start us, length us, event | category | flops | bytes accessed | tf_op | source)
XLA Modules:
  0.0 30.5 jit_solution(13478546828693011564)
XLA Ops:
  0.6 2.2 %prep.1 = (bf16[64,32,128]{2,1,0:T(8,128)(2,1)S(1)}, bf16[16,136,128]{2,1,0:T(8,128)(2,1)}) custom-call(s32[32]{0:T(128)} %rows_hbm.1, s32[32]{0:T(128)} %owner_hbm.1, bf16[64,32,128]{2,1,0:T(8,128)(2,1)} %field_hbm.1, s32[32,64]{1,0:T(8,128)} %bitcast.2), custom_call_target="tpu_custom_call" | custom-call | flops 1000000 | bytes 2000000 | tf_op jit(solution)/shard_map/prep/pallas_call | solution.py:122
  2.9 0.1 collective-permute-start
  3.0 6.0 %all-to-all-start = ((bf16[16,136,128]{2,1,0:T(8,128)(2,1)}), bf16[16,136,128]{2,1,0:T(8,128)(2,1)S(1)}, u32[]{:S(2)}, u32[]{:S(2)}) async-start(bf16[16,136,128]{2,1,0:T(8,128)(2,1)} %get-tuple-element.12), calls=%async_computation | async-start | bytes 1114112 | tf_op jit(solution)/shard_map/all_to_all | solution.py:327
  9.0 0.0 copy-start
  9.0 0.0 copy-start.1
  9.1 0.4 %collective-permute-start.2 = (bf16[32,32,128]{2,1,0:T(8,128)(2,1)S(1)}, bf16[32,32,128]{2,1,0:T(8,128)(2,1)S(1)}, u32[]{:S(2)}, u32[]{:S(2)}) collective-permute-start(bf16[32,32,128]{2,1,0:T(8,128)(2,1)S(1)} %get-tuple-element.14), channel_id=1, source_target_pairs={{0,1},{1,0},{2,3},{3,2},{4,5},{5,4},{6,7},{7,6},{8,9},{9,8},{10,11... | collective-permute-start | bytes 786440 | tf_op jit(solution)/shard_map/ppermute | solution.py:325
  9.5 0.0 copy-start.2
  9.5 0.0 copy-start.3
  9.5 0.1 collective-permute-start.1
  9.6 1.0 %collective-permute-done.2.lower_ref = bf16[32,32,128]{2,1,0:T(8,128)(2,1)S(1)} collective-permute-done((bf16[32,32,128]{2,1,0:T(8,128)(2,1)S(1)}, bf16[32,32,128]{2,1,0:T(8,128)(2,1)S(1)}, u32[]{:S(2)}, u32[]{:S(2)}) %collective-permute-start.2) | collective-permute-done | bytes 262176 | tf_op jit(solution)/shard_map/ppermute | solution.py:325
  10.7 0.4 %collective-permute-done.1.upper_ref = bf16[32,32,128]{2,1,0:T(8,128)(2,1)S(1)} collective-permute-done((bf16[32,32,128]{2,1,0:T(8,128)(2,1)S(1)}, bf16[32,32,128]{2,1,0:T(8,128)(2,1)S(1)}, u32[]{:S(2)}, u32[]{:S(2)}) %collective-permute-start.1) | collective-permute-done | bytes 262176 | tf_op jit(solution)/shard_map/ppermute | solution.py:325
  11.0 0.0 copy-done
  11.0 0.0 copy-done.1
  11.0 0.0 copy-done.2
  11.0 0.0 copy-done.3
  11.1 0.0 copy-start.4
  11.1 0.0 copy-start.5
  11.1 0.7 %side.1 = (f32[64,32]{1,0:T(8,128)S(1)}, bf16[64,32,128]{2,1,0:T(8,128)(2,1)S(1)}, f32[16,128]{1,0:T(8,128)S(1)}, bf16[256,160]{1,0:T(8,128)(2,1)S(1)}) custom-call(f32[31]{0:T(128)S(1)} %copy-done.2, s32[32,64]{1,0:T(8,128)S(1)} %bitcast.3, bf16[32,32,128]{2,1,0:T(8,128)(2,1)S(1)} %collective-permute-done.1.upper_ref, ...), custom_call_target="tpu_custom_call" | custom-call | flops 1000000 | bytes 1000000 | tf_op jit(solution)/shard_map/side/pallas_call | solution.py:174
  11.8 4.4 %collective-permute-done.cross_ref = bf16[64,32,128]{2,1,0:T(8,128)(2,1)S(1)} collective-permute-done((bf16[64,32,128]{2,1,0:T(8,128)(2,1)S(1)}, bf16[64,32,128]{2,1,0:T(8,128)(2,1)S(1)}, u32[]{:S(2)}, u32[]{:S(2)}) %collective-permute-start) | collective-permute-done | bytes 524320 | tf_op jit(solution)/shard_map/ppermute | solution.py:323
  16.2 0.0 copy-done.4
  16.2 0.0 copy-done.5
  16.2 3.9 %tile.1 = bf16[64,32,128]{2,1,0:T(8,128)(2,1)} custom-call(bf16[64,32,128]{2,1,0:T(8,128)(2,1)S(1)} %get-tuple-element.8.own_ref, bf16[64,32,128]{2,1,0:T(8,128)(2,1)S(1)} %collective-permute-done.cross_ref, bf16[64,32,128]{2,1,0:T(8,128)(2,1)S(1)} %get-tuple-element.9.near_ref, f32[64,32]{1,0:T(8,128)S(1)} %get-tuple-element.10.mask_ref, ...), custom_call_target="tpu_custom_call" | custom-call | flops 7000000000 | bytes 3000000 | tf_op jit(solution)/shard_map/tile/pallas_call | solution.py:208
  20.1 6.3 %all-to-all-done.recv_ref = bf16[16,136,128]{2,1,0:T(8,128)(2,1)S(1)} async-done(((bf16[16,136,128]{2,1,0:T(8,128)(2,1)}), bf16[16,136,128]{2,1,0:T(8,128)(2,1)S(1)}, u32[]{:S(2)}, u32[]{:S(2)}) %all-to-all-start) | async-done | bytes 557088 | tf_op jit(solution)/shard_map/all_to_all | solution.py:327
  26.4 4.1 %polar.1 = bf16[4,512,128]{2,1,0:T(8,128)(2,1)} custom-call(bf16[16,136,128]{2,1,0:T(8,128)(2,1)S(1)} %all-to-all-done.recv_ref, bf16[256,160]{1,0:T(8,128)(2,1)S(1)} %get-tuple-element.13.bands_ref, f32[16,128]{1,0:T(8,128)S(1)} %get-tuple-element.11.table_ref, bf16[128,512]{1,0:T(8,128)(2,1)S(1)} %copy-done.4, bf16[512,128]{1,0:T(8,128)(2,1)S(1)} %copy-done.5), custom_call_target="tpu_custom_call" | custom-call | flops 600000000 | bytes 2000000 | tf_op jit(solution)/shard_map/polar/pallas_call | solution.py:290
  (1 shorter events, 0.0 us)
Async XLA Ops:
  2.9 13.3 %collective-permute-start = (bf16[64,32,128]{2,1,0:T(8,128)(2,1)S(1)}, bf16[64,32,128]{2,1,0:T(8,128)(2,1)S(1)}, u32[]{:S(2)}, u32[]{:S(2)}) collective-permute-start(bf16[64,32,128]{2,1,0:T(8,128)(2,1)S(1)} %get-tuple-element.8.own_ref), channel_id=1, source_target_pairs={{0,15},{1,2},{2,1},{3,4},{4,3},{5,6},{6,5},{7,8},{8,7},{9,10},{10,... | collective-permute-start | bytes 1572872 | tf_op jit(solution)/shard_map/ppermute | solution.py:323
  3.0 23.5 %all-to-all-start = ((bf16[16,136,128]{2,1,0:T(8,128)(2,1)}), bf16[16,136,128]{2,1,0:T(8,128)(2,1)S(1)}, u32[]{:S(2)}, u32[]{:S(2)}) async-start(bf16[16,136,128]{2,1,0:T(8,128)(2,1)} %get-tuple-element.12), calls=%async_computation | async-start | bytes 1114112 | tf_op jit(solution)/shard_map/all_to_all | solution.py:327
  9.0 2.0 %copy-start = (s32[64,32]{0,1:T(8,128)S(1)}, s32[64,32]{0,1:T(8,128)}, u32[]{:S(2)}) copy-start(s32[64,32]{0,1:T(8,128)} %param.10) | copy-start | bytes 24580
  9.0 2.0 %copy-start.1 = (f32[15,128]{1,0:T(8,128)S(1)}, f32[15,128]{1,0:T(8,128)}, u32[]{:S(2)}) copy-start(f32[15,128]{1,0:T(8,128)} %taps_ref.1) | copy-start | bytes 23044
  9.1 1.6 %collective-permute-start.2 = (bf16[32,32,128]{2,1,0:T(8,128)(2,1)S(1)}, bf16[32,32,128]{2,1,0:T(8,128)(2,1)S(1)}, u32[]{:S(2)}, u32[]{:S(2)}) collective-permute-start(bf16[32,32,128]{2,1,0:T(8,128)(2,1)S(1)} %get-tuple-element.14), channel_id=1, source_target_pairs={{0,1},{1,0},{2,3},{3,2},{4,5},{5,4},{6,7},{7,6},{8,9},{9,8},{10,11... | collective-permute-start | bytes 786440 | tf_op jit(solution)/shard_map/ppermute | solution.py:325
  9.5 1.6 %copy-start.2 = (f32[31]{0:T(128)S(1)}, f32[31]{0:T(128)}, u32[]{:S(2)}) copy-start(f32[31]{0:T(128)} %polar_taps_ref.1) | copy-start | bytes 376
  9.5 1.6 %copy-start.3 = (f32[128]{0:T(128)S(1)}, f32[128]{0:T(128)}, u32[]{:S(2)}) copy-start(f32[128]{0:T(128)} %param.12) | copy-start | bytes 1540
  9.5 1.5 %collective-permute-start.1 = (bf16[32,32,128]{2,1,0:T(8,128)(2,1)S(1)}, bf16[32,32,128]{2,1,0:T(8,128)(2,1)S(1)}, u32[]{:S(2)}, u32[]{:S(2)}) collective-permute-start(bf16[32,32,128]{2,1,0:T(8,128)(2,1)S(1)} %get-tuple-element.15), channel_id=1, source_target_pairs={{0,1},{1,0},{2,3},{3,2},{4,5},{5,4},{6,7},{7,6},{8,9},{9,8},{10,11... | collective-permute-start | bytes 786440 | tf_op jit(solution)/shard_map/ppermute | solution.py:325
  11.1 5.2 %copy-start.4 = (bf16[128,512]{1,0:T(8,128)(2,1)S(1)}, bf16[128,512]{1,0:T(8,128)(2,1)}, u32[]{:S(2)}) copy-start(bf16[128,512]{1,0:T(8,128)(2,1)} %up_ref.3) | copy-start | bytes 393220
  11.1 5.2 %copy-start.5 = (bf16[512,128]{1,0:T(8,128)(2,1)S(1)}, bf16[512,128]{1,0:T(8,128)(2,1)}, u32[]{:S(2)}) copy-start(bf16[512,128]{1,0:T(8,128)(2,1)} %down_ref.3) | copy-start | bytes 393220

commit v7 on v6

--- a/solution.py
+++ b/solution.py
@@ -9,7 +9,7 @@
 
 DILATION_STEP = 4
 EXTRA = 8
-TILE_FLOPS = 7 * 10**9
+TILE_FLOPS = 11 * 10**9
 PARTS = 1
 SHARES = 2
 VMEM_BYTES = 48 * 1024 * 1024
@@ -63,7 +63,7 @@
 
 
 def prep_kernel(
-    slots, rows_hbm, owner_hbm, field_hbm, mask_hbm, masked, out_hbm,
+    slots, halo, rows_hbm, owner_hbm, field_hbm, mask_hbm, masked, edge, out_hbm,
     rows, owners, count, field, mask_t, mask_f, extra, extra_half, small_sems, load_sem, row_sems, extra_sem,
 ):
     lat_rows, cols, channels = field.shape
@@ -110,23 +110,33 @@
     masked[...] = field[...] * wide
     for e, place in enumerate(places):
         row_copy(e, *place).start()
+    odd = lax.rem(lax.axis_index("lon"), 2)
+
+    def pack(start):
+        for g in range(lat_rows // 4):
+            parts = [masked[g * 4 + q].astype(F32)[start : start + halo] for q in range(4)]
+            edge[g] = jnp.concatenate(parts, axis=0).astype(BF16)
+
+    pl.when(odd == 0)(functools.partial(pack, 0))
+    pl.when(odd == 1)(functools.partial(pack, cols - halo))
     for e, place in enumerate(places):
         row_copy(e, *place).wait()
     extra_copy.wait()
 
 
-def prep(field, land_mask, polar_rows, polar_owner, tiles, slots):
+def prep(field, land_mask, polar_rows, polar_owner, tiles, slots, halo):
     lat_rows, cols, channels = field.shape
     hbm = pl.BlockSpec(memory_space=pltpu.HBM)
     vmem = pl.BlockSpec(memory_space=pltpu.VMEM)
     return pl.pallas_call(
-        functools.partial(prep_kernel, slots),
+        functools.partial(prep_kernel, slots, halo),
         out_shape=(
             pltpu.VMEM(field.shape, BF16),
+            pltpu.VMEM((lat_rows // 4, 4 * halo, channels), BF16),
             jax.ShapeDtypeStruct((tiles, slots * cols + EXTRA, channels), BF16),
         ),
         in_specs=[hbm] * 4,
-        out_specs=(vmem, hbm),
+        out_specs=(vmem, vmem, hbm),
         scratch_shapes=[
             pltpu.SMEM(polar_rows.shape, jnp.int32),
             pltpu.SMEM(polar_owner.shape, jnp.int32),
@@ -192,15 +202,30 @@
     odd = lax.rem(lax.axis_index("lon"), 2)
 
     def all_rows(left, right):
-        triples = [(left[r], own_ref[r], right[r]) for r in range(lat_rows)]
+        triples = [(left(r), own_ref[r].astype(F32), right(r)) for r in range(lat_rows)]
         branch = branch_rows(triples, table_ref[...], up_ref[...], down_ref[...])
         wide = spread_mask(mask_ref[...], channels)
         own = own_ref[...].reshape(lat_rows * cols, channels).astype(F32)
         mixed = wide * (own + branch.astype(BF16).astype(F32))
         mixed_ref[...] = mixed.astype(BF16).reshape(lat_rows, cols, channels)
 
-    pl.when(odd == 0)(functools.partial(all_rows, cross_ref, near_ref))
-    pl.when(odd == 1)(functools.partial(all_rows, near_ref, cross_ref))
+    halo = cross_ref.shape[1] // 4
+    rest = jnp.zeros((cols - halo, channels), F32)
+
+    def near(r):
+        return near_ref[r].astype(F32)
+
+    def far(r):
+        return cross_ref[r // 4].astype(F32)[r % 4 * halo : (r % 4 + 1) * halo]
+
+    def far_left(r):
+        return jnp.concatenate([rest, far(r)], axis=0)
+
+    def far_right(r):
+        return jnp.concatenate([far(r), rest], axis=0)
+
+    pl.when(odd == 0)(functools.partial(all_rows, far_left, near))
+    pl.when(odd == 1)(functools.partial(all_rows, near, far_right))
 
 
 def tile_part(masked, cross, near, mask_f, weights):
@@ -317,10 +342,11 @@
     lat_rows, cols, channels = field.shape
     tiles = lax.axis_size("lon")
     slots = max(2, lat_rows // tiles)
-    masked, outgoing = prep(field, land_mask, polar_rows, polar_owner, tiles, slots)
+    halo = zonal_tap_weight.shape[0] // 2 * DILATION_STEP
+    masked, edge, outgoing = prep(field, land_mask, polar_rows, polar_owner, tiles, slots, halo)
     swap_pairs = [(i, i ^ 1) for i in range(tiles)]
     cross_pairs = [(i, (i + 1) % tiles if i % 2 else (i - 1) % tiles) for i in range(tiles)]
-    cross = lax.ppermute(masked, "lon", cross_pairs)
+    cross = lax.ppermute(edge, "lon", cross_pairs)
     half = lat_rows // 2
     swaps = [lax.ppermute(masked[:half], "lon", swap_pairs), lax.ppermute(masked[half:], "lon", swap_pairs)]
     order = [(lead(tiles) + i) % tiles for i in range(tiles)]

time: 30.8 us -> 30.1 us (0.977)
  waiting for transfers between devices: 12.1 us -> 10.6 us
  local copies, waits for them, and re-layouts: 0.07 us -> 0.67 us
    ppermute x1, waiting for transfers between devices: 4.42 us -> 2.91 us  [body(): cross = lax.ppermute(edge, 'lon', cross_pairs)]
    all_to_all x1, waiting for transfers between devices: 6.29 us -> 7.73 us  [body(): lax.all_to_all(outgoing, 'lon', split_axis=0, concat_axis=0, axis_index_g...]
    ppermute x1, waiting for transfers between devices: 1.02 us -> 0.01 us  [body(): lax.ppermute(masked[half:], 'lon', swap_pairs)]
    unnamed x12, local copies, waits for them, and re-layouts: 0.03 us -> 0.63 us
    ppermute x1, waiting for transfers between devices: 0.37 us -> 0.01 us  [body(): lax.ppermute(masked[:half], 'lon', swap_pairs)]
    ppermute x1, starting transfers between devices: 0.43 us -> 0.74 us  [body(): lax.ppermute(masked[half:], 'lon', swap_pairs)]
  transfers between devices with their start and end apart: 4 -> 4, of which waited for: 4 -> 2; matrix products, arithmetic and copies ran while one was open for 0% -> 0% of each run, Pallas kernels for 15% -> 16%
where the time goes in v7:
time: 30.1 us; the launch traced here: 29.8 us
  Pallas kernels  11 us (37%)
  waiting for transfers between devices  10.6 us (35%)
  starting transfers between devices  6.81 us (23%)
  between operations  0.71 us (2%)
  local copies, waits for them, and re-layouts  0.67 us (2%)
    all_to_all x1, waiting for transfers between devices, body(): lax.all_to_all(outgoing, 'lon', split_axis=0, concat_axis=0, axis_index_g...  7.73 us
    all_to_all x1, starting transfers between devices, body(): lax.all_to_all(outgoing, 'lon', split_axis=0, concat_axis=0, axis_index_g...  5.92 us
    pallas_call x1, Pallas kernels, polar_part(): pl.pallas_call(functools.partial(polar_kernel, slots, cols), out_shape=ja...  4.11 us
    pallas_call x1, Pallas kernels, tile_part(): pl.pallas_call(tile_kernel, out_shape=jax.ShapeDtypeStruct(masked.shape,...  3.95 us
    ppermute x1, waiting for transfers between devices, body(): cross = lax.ppermute(edge, 'lon', cross_pairs)  2.91 us
    pallas_call x1, Pallas kernels, prep(): pl.pallas_call(functools.partial(prep_kernel, slots, halo), out_shape=(pl...  2.25 us
    ppermute x1, starting transfers between devices, body(): lax.ppermute(masked[half:], 'lon', swap_pairs)  0.74 us
    pallas_call x1, Pallas kernels, side_part(): pl.pallas_call(side_kernel, out_shape=(jax.ShapeDtypeStruct((lat_rows, co...  0.71 us
  transfers between devices with their start and end apart: 4, of which 2 were waited for; matrix products, arithmetic and copies ran while one was open for 0% of the time, Pallas kernels for 16%

profile of v7, /device:TPU:29, one launch (start us, length us, event | category | flops | bytes accessed | tf_op | source)
XLA Modules:
  0.0 29.8 jit_solution(14612348888090735640)
XLA Ops:
  0.6 2.3 %prep.1 = (bf16[64,32,128]{2,1,0:T(8,128)(2,1)S(1)}, bf16[16,112,128]{2,1,0:T(8,128)(2,1)S(1)}, bf16[16,136,128]{2,1,0:T(8,128)(2,1)}) custom-call(s32[32]{0:T(128)} %rows_hbm.1, s32[32]{0:T(128)} %owner_hbm.1, bf16[64,32,128]{2,1,0:T(8,128)(2,1)} %field_hbm.1, s32[32,64]{1,0:T(8,128)} %bitcast.2), custom_call_target="tpu_custom_call" | custom-call | flops 1000000 | bytes 2000000 | tf_op jit(solution)/shard_map/prep/pallas_call | solution.py:131
  2.9 0.1 collective-permute-start
  3.0 0.7 %collective-permute-start.2 = (bf16[32,32,128]{2,1,0:T(8,128)(2,1)S(1)}, bf16[32,32,128]{2,1,0:T(8,128)(2,1)S(1)}, u32[]{:S(2)}, u32[]{:S(2)}) collective-permute-start(bf16[32,32,128]{2,1,0:T(8,128)(2,1)S(1)} %get-tuple-element.16), channel_id=1, source_target_pairs={{0,1},{1,0},{2,3},{3,2},{4,5},{5,4},{6,7},{7,6},{8,9},{9,8},{10,11... | collective-permute-start | bytes 786440 | tf_op jit(solution)/shard_map/ppermute | solution.py:351
  3.8 0.1 collective-permute-start.1
  3.8 0.0 copy-start
  3.8 0.0 copy-start.1
  3.8 5.9 %all-to-all-start = ((bf16[16,136,128]{2,1,0:T(8,128)(2,1)}), bf16[16,136,128]{2,1,0:T(8,128)(2,1)S(1)}, u32[]{:S(2)}, u32[]{:S(2)}) async-start(bf16[16,136,128]{2,1,0:T(8,128)(2,1)} %get-tuple-element.14), calls=%async_computation | async-start | bytes 1114112 | tf_op jit(solution)/shard_map/all_to_all | solution.py:353
  9.8 0.0 copy-start.2
  9.8 0.0 copy-start.3
  9.8 0.0 collective-permute-done.2.lower_ref
  9.8 0.0 collective-permute-done.1.upper_ref
  9.8 0.0 copy-done
  9.8 0.0 copy-done.1
  9.8 0.6 %copy-done.2 = f32[31]{0:T(128)S(1)} copy-done((f32[31]{0:T(128)S(1)}, f32[31]{0:T(128)}, u32[]{:S(2)}) %copy-start.2) | copy-done | bytes 148
  10.4 0.0 copy-done.3
  10.4 0.0 copy-start.4
  10.4 0.0 copy-start.5
  10.4 0.7 %side.1 = (f32[64,32]{1,0:T(8,128)S(1)}, bf16[64,32,128]{2,1,0:T(8,128)(2,1)S(1)}, f32[16,128]{1,0:T(8,128)S(1)}, bf16[256,160]{1,0:T(8,128)(2,1)S(1)}) custom-call(f32[31]{0:T(128)S(1)} %copy-done.2, s32[32,64]{1,0:T(8,128)S(1)} %bitcast.3, bf16[32,32,128]{2,1,0:T(8,128)(2,1)S(1)} %collective-permute-done.1.upper_ref, ...), custom_call_target="tpu_custom_call" | custom-call | flops 1000000 | bytes 1000000 | tf_op jit(solution)/shard_map/side/pallas_call | solution.py:184
  11.2 2.9 %collective-permute-done.cross_ref = bf16[16,112,128]{2,1,0:T(8,128)(2,1)S(1)} collective-permute-done((bf16[16,112,128]{2,1,0:T(8,128)(2,1)S(1)}, bf16[16,112,128]{2,1,0:T(8,128)(2,1)S(1)}, u32[]{:S(2)}, u32[]{:S(2)}) %collective-permute-start) | collective-permute-done | bytes 458784 | tf_op jit(solution)/shard_map/ppermute | solution.py:349
  14.1 0.0 copy-done.4
  14.1 0.0 copy-done.5
  14.1 3.9 %tile.1 = bf16[64,32,128]{2,1,0:T(8,128)(2,1)} custom-call(bf16[64,32,128]{2,1,0:T(8,128)(2,1)S(1)} %get-tuple-element.9.own_ref, bf16[16,112,128]{2,1,0:T(8,128)(2,1)S(1)} %collective-permute-done.cross_ref, bf16[64,32,128]{2,1,0:T(8,128)(2,1)S(1)} %get-tuple-element.11.near_ref, f32[64,32]{1,0:T(8,128)S(1)} %get-tuple-element.12.mask_ref, ...), custom_call_target="tpu_custom_call" | custom-call | flops 11000000512 | bytes 3000000 | tf_op jit(solution)/shard_map/tile/pallas_call | solution.py:233
  18.0 7.7 %all-to-all-done.recv_ref = bf16[16,136,128]{2,1,0:T(8,128)(2,1)S(1)} async-done(((bf16[16,136,128]{2,1,0:T(8,128)(2,1)}), bf16[16,136,128]{2,1,0:T(8,128)(2,1)S(1)}, u32[]{:S(2)}, u32[]{:S(2)}) %all-to-all-start) | async-done | bytes 557088 | tf_op jit(solution)/shard_map/all_to_all | solution.py:353
  25.7 4.1 %polar.1 = bf16[4,512,128]{2,1,0:T(8,128)(2,1)} custom-call(bf16[16,136,128]{2,1,0:T(8,128)(2,1)S(1)} %all-to-all-done.recv_ref, bf16[256,160]{1,0:T(8,128)(2,1)S(1)} %get-tuple-element.15.bands_ref, f32[16,128]{1,0:T(8,128)S(1)} %get-tuple-element.13.table_ref, bf16[128,512]{1,0:T(8,128)(2,1)S(1)} %copy-done.4, bf16[512,128]{1,0:T(8,128)(2,1)S(1)} %copy-done.5), custom_call_target="tpu_custom_call" | custom-call | flops 600000000 | bytes 2000000 | tf_op jit(solution)/shard_map/polar/pallas_call | solution.py:315
  (1 shorter events, 0.0 us)
Async XLA Ops:
  2.9 11.2 %collective-permute-start = (bf16[16,112,128]{2,1,0:T(8,128)(2,1)S(1)}, bf16[16,112,128]{2,1,0:T(8,128)(2,1)S(1)}, u32[]{:S(2)}, u32[]{:S(2)}) collective-permute-start(bf16[16,112,128]{2,1,0:T(8,128)(2,1)S(1)} %get-tuple-element.10), channel_id=1, source_target_pairs={{0,15},{1,2},{2,1},{3,4},{4,3},{5,6},{6,5},{7,8},{8,7},{9,10},{10,... | collective-permute-start | bytes 1376264 | tf_op jit(solution)/shard_map/ppermute | solution.py:349
  3.0 6.8 %collective-permute-start.2 = (bf16[32,32,128]{2,1,0:T(8,128)(2,1)S(1)}, bf16[32,32,128]{2,1,0:T(8,128)(2,1)S(1)}, u32[]{:S(2)}, u32[]{:S(2)}) collective-permute-start(bf16[32,32,128]{2,1,0:T(8,128)(2,1)S(1)} %get-tuple-element.16), channel_id=1, source_target_pairs={{0,1},{1,0},{2,3},{3,2},{4,5},{5,4},{6,7},{7,6},{8,9},{9,8},{10,11... | collective-permute-start | bytes 786440 | tf_op jit(solution)/shard_map/ppermute | solution.py:351
  3.8 6.0 %collective-permute-start.1 = (bf16[32,32,128]{2,1,0:T(8,128)(2,1)S(1)}, bf16[32,32,128]{2,1,0:T(8,128)(2,1)S(1)}, u32[]{:S(2)}, u32[]{:S(2)}) collective-permute-start(bf16[32,32,128]{2,1,0:T(8,128)(2,1)S(1)} %get-tuple-element.17), channel_id=1, source_target_pairs={{0,1},{1,0},{2,3},{3,2},{4,5},{5,4},{6,7},{7,6},{8,9},{9,8},{10,11... | collective-permute-start | bytes 786440 | tf_op jit(solution)/shard_map/ppermute | solution.py:351
  3.8 6.0 %copy-start = (s32[64,32]{0,1:T(8,128)S(1)}, s32[64,32]{0,1:T(8,128)}, u32[]{:S(2)}) copy-start(s32[64,32]{0,1:T(8,128)} %param.10) | copy-start | bytes 24580
  3.8 6.0 %copy-start.1 = (f32[15,128]{1,0:T(8,128)S(1)}, f32[15,128]{1,0:T(8,128)}, u32[]{:S(2)}) copy-start(f32[15,128]{1,0:T(8,128)} %taps_ref.1) | copy-start | bytes 23044
  3.8 21.9 %all-to-all-start = ((bf16[16,136,128]{2,1,0:T(8,128)(2,1)}), bf16[16,136,128]{2,1,0:T(8,128)(2,1)S(1)}, u32[]{:S(2)}, u32[]{:S(2)}) async-start(bf16[16,136,128]{2,1,0:T(8,128)(2,1)} %get-tuple-element.14), calls=%async_computation | async-start | bytes 1114112 | tf_op jit(solution)/shard_map/all_to_all | solution.py:353
  9.8 0.7 %copy-start.2 = (f32[31]{0:T(128)S(1)}, f32[31]{0:T(128)}, u32[]{:S(2)}) copy-start(f32[31]{0:T(128)} %polar_taps_ref.1) | copy-start | bytes 376
  9.8 0.7 %copy-start.3 = (f32[128]{0:T(128)S(1)}, f32[128]{0:T(128)}, u32[]{:S(2)}) copy-start(f32[128]{0:T(128)} %param.12) | copy-start | bytes 1540
  10.4 3.6 %copy-start.4 = (bf16[128,512]{1,0:T(8,128)(2,1)S(1)}, bf16[128,512]{1,0:T(8,128)(2,1)}, u32[]{:S(2)}) copy-start(bf16[128,512]{1,0:T(8,128)(2,1)} %up_ref.3) | copy-start | bytes 393220
  10.4 3.6 %copy-start.5 = (bf16[512,128]{1,0:T(8,128)(2,1)S(1)}, bf16[512,128]{1,0:T(8,128)(2,1)}, u32[]{:S(2)}) copy-start(bf16[512,128]{1,0:T(8,128)(2,1)} %down_ref.3) | copy-start | bytes 393220

commit v8 on v7

--- a/solution.py
+++ b/solution.py
@@ -9,7 +9,7 @@
 
 DILATION_STEP = 4
 EXTRA = 8
-TILE_FLOPS = 11 * 10**9
+TILE_FLOPS = 9 * 10**9
 PARTS = 1
 SHARES = 2
 VMEM_BYTES = 48 * 1024 * 1024
@@ -59,7 +59,7 @@
 
 
 def lead(tiles):
-    return tiles * 7 // 16
+    return tiles * 9 // 16
 
 
 def prep_kernel(
@@ -157,11 +157,11 @@
     )(polar_rows, polar_owner, field, land_mask.T)
 
 
-def side_kernel(polar_taps_ref, mask_ref, upper_ref, lower_ref, taps_ref, gain_ref, mask_f, near, table, bands_ref):
-    half = upper_ref.shape[0]
+def side_kernel(polar_taps_ref, mask_ref, first_ref, second_ref, third_ref, fourth_ref, taps_ref, gain_ref, mask_f, near, table, bands_ref):
+    part = first_ref.shape[0]
     mask_f[...] = mask_ref[...].astype(F32).T
-    near[:half] = upper_ref[...]
-    near[half:] = lower_ref[...]
+    for p, ref in enumerate((first_ref, second_ref, third_ref, fourth_ref)):
+        near[p * part : (p + 1) * part] = ref[...]
     table[: taps_ref.shape[0]] = taps_ref[...]
     table[taps_ref.shape[0] :] = gain_ref[...]
     n, depth = bands_ref.shape[0] // 2, bands_ref.shape[1]
@@ -180,16 +180,16 @@
     lat_rows, cols = land_mask.shape
     smem = pl.BlockSpec(memory_space=pltpu.SMEM)
     vmem = pl.BlockSpec(memory_space=pltpu.VMEM)
-    half, _, channels = swaps[0].shape
+    part, _, channels = swaps[0].shape
     return pl.pallas_call(
         side_kernel,
         out_shape=(
             jax.ShapeDtypeStruct((lat_rows, cols), F32),
-            jax.ShapeDtypeStruct((2 * half, cols, channels), BF16),
+            jax.ShapeDtypeStruct((4 * part, cols, channels), BF16),
             jax.ShapeDtypeStruct((zonal_tap_weight.shape[0] + 1, channels), F32),
             jax.ShapeDtypeStruct((256, 160), BF16),
         ),
-        in_specs=[smem] + [vmem] * 5,
+        in_specs=[smem] + [vmem] * 7,
         out_specs=(vmem,) * 4,
         compiler_params=pltpu.CompilerParams(vmem_limit_bytes=VMEM_BYTES),
         cost_estimate=pl.CostEstimate(flops=10**6, bytes_accessed=10**6, transcendentals=0),
@@ -347,8 +347,8 @@
     swap_pairs = [(i, i ^ 1) for i in range(tiles)]
     cross_pairs = [(i, (i + 1) % tiles if i % 2 else (i - 1) % tiles) for i in range(tiles)]
     cross = lax.ppermute(edge, "lon", cross_pairs)
-    half = lat_rows // 2
-    swaps = [lax.ppermute(masked[:half], "lon", swap_pairs), lax.ppermute(masked[half:], "lon", swap_pairs)]
+    part = lat_rows // 4
+    swaps = [lax.ppermute(masked[p * part : (p + 1) * part], "lon", swap_pairs) for p in range(4)]
     order = [(lead(tiles) + i) % tiles for i in range(tiles)]
     recv = lax.all_to_all(
         outgoing, "lon", split_axis=0, concat_axis=0, axis_index_groups=[order], tiled=True

time: 30.1 us -> 30.1 us (level)
  local copies, waits for them, and re-layouts: 0.67 us -> 0.07 us
  starting transfers between devices: 6.81 us -> 7.19 us
    ppermute x2 -> x4, waiting for transfers between devices: 0.01 us -> 1.2 us  [body(): lax.ppermute(masked[p * part:(p + 1) * part], 'lon', swap_pairs)]
    all_to_all x1, waiting for transfers between devices: 7.73 us -> 6.92 us  [body(): lax.all_to_all(outgoing, 'lon', split_axis=0, concat_axis=0, axis_index_g...]
    unnamed x12, local copies, waits for them, and re-layouts: 0.63 us -> 0.03 us
    ppermute x2 -> x4, starting transfers between devices: 0.82 us -> 1.09 us  [body(): lax.ppermute(masked[p * part:(p + 1) * part], 'lon', swap_pairs)]
  transfers between devices with their start and end apart: 4 -> 6, of which waited for: 2 -> 6; matrix products, arithmetic and copies ran while one was open for 0% -> 0% of each run, Pallas kernels for 16% -> 16%
where the time goes in v8:
time: 30.1 us; the launch traced here: 29.9 us
  Pallas kernels  11.1 us (37%)
  waiting for transfers between devices  10.9 us (36%)
  starting transfers between devices  7.19 us (24%)
  between operations  0.71 us (2%)
    all_to_all x1, waiting for transfers between devices, body(): lax.all_to_all(outgoing, 'lon', split_axis=0, concat_axis=0, axis_index_g...  6.92 us
    all_to_all x1, starting transfers between devices, body(): lax.all_to_all(outgoing, 'lon', split_axis=0, concat_axis=0, axis_index_g...  6.04 us
    pallas_call x1, Pallas kernels, polar_part(): pl.pallas_call(functools.partial(polar_kernel, slots, cols), out_shape=ja...  4.12 us
    pallas_call x1, Pallas kernels, tile_part(): pl.pallas_call(tile_kernel, out_shape=jax.ShapeDtypeStruct(masked.shape,...  3.96 us
    ppermute x1, waiting for transfers between devices, body(): cross = lax.ppermute(edge, 'lon', cross_pairs)  2.73 us
    pallas_call x1, Pallas kernels, prep(): pl.pallas_call(functools.partial(prep_kernel, slots, halo), out_shape=(pl...  2.25 us
    ppermute x4, waiting for transfers between devices, body(): lax.ppermute(masked[p * part:(p + 1) * part], 'lon', swap_pairs)  1.2 us
    ppermute x4, starting transfers between devices, body(): lax.ppermute(masked[p * part:(p + 1) * part], 'lon', swap_pairs)  1.09 us
  transfers between devices with their start and end apart: 6, of which 6 were waited for; matrix products, arithmetic and copies ran while one was open for 0% of the time, Pallas kernels for 16%

profile of v8, /device:TPU:29, one launch (start us, length us, event | category | flops | bytes accessed | tf_op | source)
XLA Modules:
  0.0 29.9 jit_solution(9155134408704425015)
XLA Ops:
  0.6 2.2 %prep.1 = (bf16[64,32,128]{2,1,0:T(8,128)(2,1)S(1)}, bf16[16,112,128]{2,1,0:T(8,128)(2,1)S(1)}, bf16[16,136,128]{2,1,0:T(8,128)(2,1)}) custom-call(s32[32]{0:T(128)} %rows_hbm.1, s32[32]{0:T(128)} %owner_hbm.1, bf16[64,32,128]{2,1,0:T(8,128)(2,1)} %field_hbm.1, s32[32,64]{1,0:T(8,128)} %bitcast.2), custom_call_target="tpu_custom_call" | custom-call | flops 1000000 | bytes 2000000 | tf_op jit(solution)/shard_map/prep/pallas_call | solution.py:131
  2.9 0.1 collective-permute-start
  3.0 6.0 %all-to-all-start = ((bf16[16,136,128]{2,1,0:T(8,128)(2,1)}), bf16[16,136,128]{2,1,0:T(8,128)(2,1)S(1)}, u32[]{:S(2)}, u32[]{:S(2)}) async-start(bf16[16,136,128]{2,1,0:T(8,128)(2,1)} %get-tuple-element.14), calls=%async_computation | async-start | bytes 1114112 | tf_op jit(solution)/shard_map/all_to_all | solution.py:353
  9.0 0.0 copy-start
  9.1 0.0 copy-start.1
  9.1 0.4 %collective-permute-start.4 = (bf16[16,32,128]{2,1,0:T(8,128)(2,1)S(1)}, bf16[16,32,128]{2,1,0:T(8,128)(2,1)S(1)}, u32[]{:S(2)}, u32[]{:S(2)}) collective-permute-start(bf16[16,32,128]{2,1,0:T(8,128)(2,1)S(1)} %get-tuple-element.16), channel_id=1, source_target_pairs={{0,1},{1,0},{2,3},{3,2},{4,5},{5,4},{6,7},{7,6},{8,9},{9,8},{10,11... | collective-permute-start | bytes 393224 | tf_op jit(solution)/shard_map/ppermute | solution.py:351
  9.5 0.1 collective-permute-start.3
  9.6 0.4 %collective-permute-start.2 = (bf16[16,32,128]{2,1,0:T(8,128)(2,1)S(1)}, bf16[16,32,128]{2,1,0:T(8,128)(2,1)S(1)}, u32[]{:S(2)}, u32[]{:S(2)}) collective-permute-start(bf16[16,32,128]{2,1,0:T(8,128)(2,1)S(1)} %get-tuple-element.18), channel_id=1, source_target_pairs={{0,1},{1,0},{2,3},{3,2},{4,5},{5,4},{6,7},{7,6},{8,9},{9,8},{10,11... | collective-permute-start | bytes 393224 | tf_op jit(solution)/shard_map/ppermute | solution.py:351
  10.0 0.0 copy-start.2
  10.0 0.0 copy-start.3
  10.0 0.1 collective-permute-start.1
  10.2 0.3 %collective-permute-done.4.fourth_ref = bf16[16,32,128]{2,1,0:T(8,128)(2,1)S(1)} collective-permute-done((bf16[16,32,128]{2,1,0:T(8,128)(2,1)S(1)}, bf16[16,32,128]{2,1,0:T(8,128)(2,1)S(1)}, u32[]{:S(2)}, u32[]{:S(2)}) %collective-permute-start.4) | collective-permute-done | bytes 131104 | tf_op jit(solution)/shard_map/ppermute | solution.py:351
  10.5 0.4 %collective-permute-done.3.third_ref = bf16[16,32,128]{2,1,0:T(8,128)(2,1)S(1)} collective-permute-done((bf16[16,32,128]{2,1,0:T(8,128)(2,1)S(1)}, bf16[16,32,128]{2,1,0:T(8,128)(2,1)S(1)}, u32[]{:S(2)}, u32[]{:S(2)}) %collective-permute-start.3) | collective-permute-done | bytes 131104 | tf_op jit(solution)/shard_map/ppermute | solution.py:351
  10.8 0.2 collective-permute-done.2.second_ref
  11.0 0.3 %collective-permute-done.1.first_ref = bf16[16,32,128]{2,1,0:T(8,128)(2,1)S(1)} collective-permute-done((bf16[16,32,128]{2,1,0:T(8,128)(2,1)S(1)}, bf16[16,32,128]{2,1,0:T(8,128)(2,1)S(1)}, u32[]{:S(2)}, u32[]{:S(2)}) %collective-permute-start.1) | collective-permute-done | bytes 131104 | tf_op jit(solution)/shard_map/ppermute | solution.py:351
  11.4 0.0 copy-done
  11.4 0.0 copy-done.1
  11.4 0.0 copy-done.2
  11.4 0.0 copy-done.3
  11.4 0.0 copy-start.4
  11.4 0.0 copy-start.5
  11.4 0.7 %side.1 = (f32[64,32]{1,0:T(8,128)S(1)}, bf16[64,32,128]{2,1,0:T(8,128)(2,1)S(1)}, f32[16,128]{1,0:T(8,128)S(1)}, bf16[256,160]{1,0:T(8,128)(2,1)S(1)}) custom-call(f32[31]{0:T(128)S(1)} %copy-done.2, s32[32,64]{1,0:T(8,128)S(1)} %bitcast.3, bf16[16,32,128]{2,1,0:T(8,128)(2,1)S(1)} %collective-permute-done.1.first_ref, ...), custom_call_target="tpu_custom_call" | custom-call | flops 1000000 | bytes 1000000 | tf_op jit(solution)/shard_map/side/pallas_call | solution.py:184
  12.1 2.7 %collective-permute-done.cross_ref = bf16[16,112,128]{2,1,0:T(8,128)(2,1)S(1)} collective-permute-done((bf16[16,112,128]{2,1,0:T(8,128)(2,1)S(1)}, bf16[16,112,128]{2,1,0:T(8,128)(2,1)S(1)}, u32[]{:S(2)}, u32[]{:S(2)}) %collective-permute-start) | collective-permute-done | bytes 458784 | tf_op jit(solution)/shard_map/ppermute | solution.py:349
  14.9 0.0 copy-done.4
  14.9 0.0 copy-done.5
  14.9 4.0 %tile.1 = bf16[64,32,128]{2,1,0:T(8,128)(2,1)} custom-call(bf16[64,32,128]{2,1,0:T(8,128)(2,1)S(1)} %get-tuple-element.9.own_ref, bf16[16,112,128]{2,1,0:T(8,128)(2,1)S(1)} %collective-permute-done.cross_ref, bf16[64,32,128]{2,1,0:T(8,128)(2,1)S(1)} %get-tuple-element.11.near_ref, f32[64,32]{1,0:T(8,128)S(1)} %get-tuple-element.12.mask_ref, ...), custom_call_target="tpu_custom_call" | custom-call | flops 8999999488 | bytes 3000000 | tf_op jit(solution)/shard_map/tile/pallas_call | solution.py:233
  18.8 6.9 %all-to-all-done.recv_ref = bf16[16,136,128]{2,1,0:T(8,128)(2,1)S(1)} async-done(((bf16[16,136,128]{2,1,0:T(8,128)(2,1)}), bf16[16,136,128]{2,1,0:T(8,128)(2,1)S(1)}, u32[]{:S(2)}, u32[]{:S(2)}) %all-to-all-start) | async-done | bytes 557088 | tf_op jit(solution)/shard_map/all_to_all | solution.py:353
  25.8 4.1 %polar.1 = bf16[4,512,128]{2,1,0:T(8,128)(2,1)} custom-call(bf16[16,136,128]{2,1,0:T(8,128)(2,1)S(1)} %all-to-all-done.recv_ref, bf16[256,160]{1,0:T(8,128)(2,1)S(1)} %get-tuple-element.15.bands_ref, f32[16,128]{1,0:T(8,128)S(1)} %get-tuple-element.13.table_ref, bf16[128,512]{1,0:T(8,128)(2,1)S(1)} %copy-done.4, bf16[512,128]{1,0:T(8,128)(2,1)S(1)} %copy-done.5), custom_call_target="tpu_custom_call" | custom-call | flops 600000000 | bytes 2000000 | tf_op jit(solution)/shard_map/polar/pallas_call | solution.py:315
  (1 shorter events, 0.0 us)
Async XLA Ops:
  2.9 12.0 %collective-permute-start = (bf16[16,112,128]{2,1,0:T(8,128)(2,1)S(1)}, bf16[16,112,128]{2,1,0:T(8,128)(2,1)S(1)}, u32[]{:S(2)}, u32[]{:S(2)}) collective-permute-start(bf16[16,112,128]{2,1,0:T(8,128)(2,1)S(1)} %get-tuple-element.10), channel_id=1, source_target_pairs={{0,15},{1,2},{2,1},{3,4},{4,3},{5,6},{6,5},{7,8},{8,7},{9,10},{10,... | collective-permute-start | bytes 1376264 | tf_op jit(solution)/shard_map/ppermute | solution.py:349
  3.0 22.8 %all-to-all-start = ((bf16[16,136,128]{2,1,0:T(8,128)(2,1)}), bf16[16,136,128]{2,1,0:T(8,128)(2,1)S(1)}, u32[]{:S(2)}, u32[]{:S(2)}) async-start(bf16[16,136,128]{2,1,0:T(8,128)(2,1)} %get-tuple-element.14), calls=%async_computation | async-start | bytes 1114112 | tf_op jit(solution)/shard_map/all_to_all | solution.py:353
  9.0 2.4 %copy-start = (s32[64,32]{0,1:T(8,128)S(1)}, s32[64,32]{0,1:T(8,128)}, u32[]{:S(2)}) copy-start(s32[64,32]{0,1:T(8,128)} %param.10) | copy-start | bytes 24580
  9.1 2.3 %copy-start.1 = (f32[15,128]{1,0:T(8,128)S(1)}, f32[15,128]{1,0:T(8,128)}, u32[]{:S(2)}) copy-start(f32[15,128]{1,0:T(8,128)} %taps_ref.1) | copy-start | bytes 23044
  9.1 1.4 %collective-permute-start.4 = (bf16[16,32,128]{2,1,0:T(8,128)(2,1)S(1)}, bf16[16,32,128]{2,1,0:T(8,128)(2,1)S(1)}, u32[]{:S(2)}, u32[]{:S(2)}) collective-permute-start(bf16[16,32,128]{2,1,0:T(8,128)(2,1)S(1)} %get-tuple-element.16), channel_id=1, source_target_pairs={{0,1},{1,0},{2,3},{3,2},{4,5},{5,4},{6,7},{7,6},{8,9},{9,8},{10,11... | collective-permute-start | bytes 393224 | tf_op jit(solution)/shard_map/ppermute | solution.py:351
  9.5 1.3 %collective-permute-start.3 = (bf16[16,32,128]{2,1,0:T(8,128)(2,1)S(1)}, bf16[16,32,128]{2,1,0:T(8,128)(2,1)S(1)}, u32[]{:S(2)}, u32[]{:S(2)}) collective-permute-start(bf16[16,32,128]{2,1,0:T(8,128)(2,1)S(1)} %get-tuple-element.17), channel_id=1, source_target_pairs={{0,1},{1,0},{2,3},{3,2},{4,5},{5,4},{6,7},{7,6},{8,9},{9,8},{10,11... | collective-permute-start | bytes 393224 | tf_op jit(solution)/shard_map/ppermute | solution.py:351
  9.6 1.4 %collective-permute-start.2 = (bf16[16,32,128]{2,1,0:T(8,128)(2,1)S(1)}, bf16[16,32,128]{2,1,0:T(8,128)(2,1)S(1)}, u32[]{:S(2)}, u32[]{:S(2)}) collective-permute-start(bf16[16,32,128]{2,1,0:T(8,128)(2,1)S(1)} %get-tuple-element.18), channel_id=1, source_target_pairs={{0,1},{1,0},{2,3},{3,2},{4,5},{5,4},{6,7},{7,6},{8,9},{9,8},{10,11... | collective-permute-start | bytes 393224 | tf_op jit(solution)/shard_map/ppermute | solution.py:351
  10.0 1.4 %copy-start.2 = (f32[31]{0:T(128)S(1)}, f32[31]{0:T(128)}, u32[]{:S(2)}) copy-start(f32[31]{0:T(128)} %polar_taps_ref.1) | copy-start | bytes 376
  10.0 1.4 %copy-start.3 = (f32[128]{0:T(128)S(1)}, f32[128]{0:T(128)}, u32[]{:S(2)}) copy-start(f32[128]{0:T(128)} %param.12) | copy-start | bytes 1540
  10.0 1.3 %collective-permute-start.1 = (bf16[16,32,128]{2,1,0:T(8,128)(2,1)S(1)}, bf16[16,32,128]{2,1,0:T(8,128)(2,1)S(1)}, u32[]{:S(2)}, u32[]{:S(2)}) collective-permute-start(bf16[16,32,128]{2,1,0:T(8,128)(2,1)S(1)} %get-tuple-element.19), channel_id=1, source_target_pairs={{0,1},{1,0},{2,3},{3,2},{4,5},{5,4},{6,7},{7,6},{8,9},{9,8},{10,11... | collective-permute-start | bytes 393224 | tf_op jit(solution)/shard_map/ppermute | solution.py:351
  11.4 3.5 %copy-start.4 = (bf16[128,512]{1,0:T(8,128)(2,1)S(1)}, bf16[128,512]{1,0:T(8,128)(2,1)}, u32[]{:S(2)}) copy-start(bf16[128,512]{1,0:T(8,128)(2,1)} %up_ref.3) | copy-start | bytes 393220
  11.4 3.5 %copy-start.5 = (bf16[512,128]{1,0:T(8,128)(2,1)S(1)}, bf16[512,128]{1,0:T(8,128)(2,1)}, u32[]{:S(2)}) copy-start(bf16[512,128]{1,0:T(8,128)(2,1)} %down_ref.3) | copy-start | bytes 393220
